TPU v7x, 32 devices: a whole 2x2x4 slice. The times are simulated.
32 devices in a mesh: shard: 4 (over z), ctx: 2 (over x), tp: 4 (over y, core).
Axes of the slice: x: 2, y: 2, z: 4, core: 2. Of those that a mesh axis runs over, the one named last changes fastest.
Arguments:
- video_tokens: bfloat16 [4, 1568, 1024], P('shard', 'ctx'), may hold values from -6 to 6
- qkv_weight: bfloat16 [1024, 3, 1024], P(('shard', 'ctx'), None, 'tp'), may hold values from -0.1875 to 0.1875
- q_bias: bfloat16 [1024], P('tp'), may hold values from -3 to 3
- v_bias: bfloat16 [1024], P('tp'), may hold values from -0.59765625 to 0.59765625
- proj_weight: bfloat16 [1024, 1024], P('tp', ('shard', 'ctx')), may hold values from -0.75 to 0.75
- proj_bias: bfloat16 [1024], replicated, may hold values from -2 to 2
- norm1_gain: bfloat16 [1024], replicated, may hold values from 0.5 to 1.5
- norm1_shift: bfloat16 [1024], replicated, may hold values from -2 to 2
- norm2_gain: bfloat16 [1024], replicated, may hold values from 0.5 to 1.5
- norm2_shift: bfloat16 [1024], replicated, may hold values from -2 to 2
- fc1_weight: bfloat16 [1024, 4096], P(('shard', 'ctx'), 'tp'), may hold values from -0.1875 to 0.1875
- fc1_bias: bfloat16 [4096], P('tp'), may hold values from -3 to 3
- fc2_weight: bfloat16 [4096, 1024], P('tp', ('shard', 'ctx')), may hold values from -0.09375 to 0.09375
- fc2_bias: bfloat16 [1024], replicated, may hold values from -2 to 2
- out_grad: bfloat16 [4, 1568, 1024], P('shard', 'ctx'), may hold values from -6 to 6
Outputs:
- layer_out: bfloat16 [4, 1568, 1024], P('shard', 'ctx')
- input_grad: bfloat16 [4, 1568, 1024], P('shard', 'ctx')
- grad_qkv_weight: float32 [1024, 3, 1024], P(('shard', 'ctx'), None, 'tp')
- grad_q_bias: float32 [1024], P('tp')
- grad_v_bias: float32 [1024], P('tp')
- grad_proj_weight: float32 [1024, 1024], P('tp', ('shard', 'ctx'))
- grad_proj_bias: float32 [1024], replicated
- grad_norm1_gain: float32 [1024], replicated
- grad_norm1_shift: float32 [1024], replicated
- grad_norm2_gain: float32 [1024], replicated
- grad_norm2_shift: float32 [1024], replicated
- grad_fc1_weight: float32 [1024, 4096], P(('shard', 'ctx'), 'tp')
- grad_fc1_bias: float32 [4096], P('tp')
- grad_fc2_weight: float32 [4096, 1024], P('tp', ('shard', 'ctx'))
- grad_fc2_bias: float32 [1024], replicated
All inputs are finite; a program needn't handle non-finite values.
Results may differ from a plain program's by a relative error of at most 0.014.
Values may be sent and summed in bfloat16 or wider, within the bound.
No kernel may reach another device: no remote copies, remote signals or barrier semaphores. Data moves between devices by JAX's collectives and lax.ppermute only.
A program may use at most 128 MiB of HBM per device.

v0:
```python
import jax
import jax.numpy as jnp
from jax import lax
from jax.sharding import PartitionSpec as P

HD = 64


norm_eps = 1e-06


def norm_rows(values, gain, shift):
    row_mean = jnp.mean(values, axis=-1, keepdims=True)
    centered = values - row_mean
    variance = jnp.mean(centered * centered, axis=-1, keepdims=True)
    return centered * lax.rsqrt(variance + norm_eps) * gain + shift


def gelu_exact(values):
    return jax.nn.gelu(values, approximate=False)


def to_heads(matrix, head_count):
    return matrix.reshape(matrix.shape[0], head_count, -1).transpose(1, 0, 2)


def from_heads(stacked):
    return stacked.transpose(1, 0, 2).reshape(stacked.shape[1], -1)


def product(left, right):
    return jnp.dot(left, right, preferred_element_type=jnp.float32)


def product_tn(left, right):
    return lax.dot_general(
        left, right, (((0,), (0,)), ((), ())), preferred_element_type=jnp.float32
    )


def product_nt(left, right):
    return lax.dot_general(
        left, right, (((1,), (1,)), ((), ())), preferred_element_type=jnp.float32
    )


def body(
    video_tokens,
    qkv_weight,
    q_bias,
    v_bias,
    proj_weight,
    proj_bias,
    norm1_gain,
    norm1_shift,
    norm2_gain,
    norm2_shift,
    fc1_weight,
    fc1_bias,
    fc2_weight,
    fc2_bias,
    out_grad,
):
    score_scale = HD ** (-0.5)
    inputs = video_tokens[0].astype(jnp.float32)
    model_width = inputs.shape[1]
    owned = (qkv_weight, proj_weight, fc1_weight, fc2_weight)
    qkv_full, proj_full, fc1_full, fc2_full = (
        lax.all_gather(owned[0], ("shard", "ctx"), axis=0, tiled=True),
        lax.all_gather(owned[1], ("shard", "ctx"), axis=1, tiled=True),
        lax.all_gather(owned[2], ("shard", "ctx"), axis=0, tiled=True),
        lax.all_gather(owned[3], ("shard", "ctx"), axis=1, tiled=True),
    )
    local_width = qkv_full.shape[2]
    head_count = local_width // HD
    qkv_flat = qkv_full.reshape(model_width, 3 * local_width)
    (
        q_bias_f,
        v_bias_f,
        proj_bias_f,
        gain_one,
        shift_one,
        gain_two,
        shift_two,
        fc1_bias_f,
        fc2_bias_f,
    ) = tuple(
        (
            param.astype(jnp.float32)
            for param in (
                q_bias,
                v_bias,
                proj_bias,
                norm1_gain,
                norm1_shift,
                norm2_gain,
                norm2_shift,
                fc1_bias,
                fc2_bias,
            )
        )
    )
    normed, norm1_pull = jax.vjp(norm_rows, inputs, gain_one, shift_one)
    normed_b = normed.astype(jnp.bfloat16)
    projected = product(normed_b, qkv_flat).reshape(-1, 3, local_width)
    queries = (projected[:, 0] + q_bias_f).astype(jnp.bfloat16)
    key_rows = projected[:, 1].astype(jnp.bfloat16)
    value_rows = (projected[:, 2] + v_bias_f).astype(jnp.bfloat16)
    key_all, value_all = (
        lax.all_gather(key_rows, "ctx", axis=0, tiled=True),
        lax.all_gather(value_rows, "ctx", axis=0, tiled=True),
    )
    heads_q = to_heads(queries, head_count)
    heads_k = to_heads(key_all, head_count)
    heads_v = to_heads(value_all, head_count)

    def head_forward(pieces):
        head_q, head_k, head_v = pieces
        scores = product_nt(head_q, head_k) * score_scale
        row_max = jnp.max(scores, axis=-1, keepdims=True)
        shifted = jnp.exp(scores - row_max)
        row_sum = jnp.sum(shifted, axis=-1, keepdims=True)
        mixture = product((shifted / row_sum).astype(jnp.bfloat16), head_v)
        return (mixture, (row_max + jnp.log(row_sum))[:, 0])

    head_mix, log_norms = lax.map(head_forward, (heads_q, heads_k, heads_v))
    mixture_b = from_heads(head_mix).astype(jnp.bfloat16)
    attn_terms = product(mixture_b, proj_full)
    middle = inputs + lax.psum(attn_terms, "tp") + proj_bias_f
    second, norm2_pull = jax.vjp(norm_rows, middle, gain_two, shift_two)
    second_b = second.astype(jnp.bfloat16)
    pre_act = product(second_b, fc1_full) + fc1_bias_f
    hidden_f, gelu_pull = jax.vjp(gelu_exact, pre_act)
    hidden_b = hidden_f.astype(jnp.bfloat16)
    mlp_terms = product(hidden_b, fc2_full)
    out_rows = (
        middle + lax.psum(mlp_terms.astype(jnp.bfloat16), "tp").astype(jnp.float32) + fc2_bias_f
    ).astype(jnp.bfloat16)
    qkv_full, proj_full, fc1_full, fc2_full = (
        lax.all_gather(owned[0], ("shard", "ctx"), axis=0, tiled=True),
        lax.all_gather(owned[1], ("shard", "ctx"), axis=1, tiled=True),
        lax.all_gather(owned[2], ("shard", "ctx"), axis=0, tiled=True),
        lax.all_gather(owned[3], ("shard", "ctx"), axis=1, tiled=True),
    )
    qkv_flat = qkv_full.reshape(model_width, 3 * local_width)
    grad_b = out_grad[0]
    grad_f = grad_b.astype(jnp.float32)
    d_fc2 = product_tn(hidden_b, grad_b)
    d_fc2_bias = jnp.sum(grad_f, axis=0)
    d_hidden = product_nt(grad_b, fc2_full)
    d_pre_b = gelu_pull(d_hidden)[0].astype(jnp.bfloat16)
    d_fc1 = product_tn(second_b, d_pre_b)
    d_fc1_bias = jnp.sum(d_pre_b.astype(jnp.float32), axis=0)
    second_terms = product_nt(d_pre_b, fc1_full)
    d_second = lax.psum(second_terms, "tp")
    d_mid_norm, d_gain_two, d_shift_two = norm2_pull(d_second)
    d_middle = grad_f + d_mid_norm
    d_middle_b = d_middle.astype(jnp.bfloat16)
    d_proj = product_tn(mixture_b, d_middle_b)
    d_proj_bias = jnp.sum(d_middle_b.astype(jnp.float32), axis=0)
    d_mixture_b = product_nt(d_middle_b, proj_full).astype(jnp.bfloat16)

    def head_backward(pieces):
        head_q, head_k, head_v, log_norm, head_grad = pieces
        scores = product_nt(head_q, head_k) * score_scale
        probs_f = jnp.exp(scores - log_norm[:, None])
        d_probs = product_nt(head_grad, head_v)
        d_value = product_tn(probs_f.astype(jnp.bfloat16), head_grad)
        row_dot = jnp.sum(probs_f * d_probs, axis=-1, keepdims=True)
        d_scores = (probs_f * (d_probs - row_dot)).astype(jnp.bfloat16)
        d_query = product(d_scores, head_k) * score_scale
        d_key = product_tn(d_scores, head_q) * score_scale
        return (d_query, d_key, d_value)

    head_dq, head_dk, head_dv = lax.map(
        head_backward, (heads_q, heads_k, heads_v, log_norms, to_heads(d_mixture_b, head_count))
    )
    d_key_sum, d_value_sum = (
        lax.psum_scatter(
            from_heads(head_dk).astype(jnp.bfloat16), "ctx", scatter_dimension=0, tiled=True
        ).astype(jnp.float32),
        lax.psum_scatter(
            from_heads(head_dv).astype(jnp.bfloat16), "ctx", scatter_dimension=0, tiled=True
        ).astype(jnp.float32),
    )
    d_query_b = from_heads(head_dq).astype(jnp.bfloat16)
    d_key_b = d_key_sum.astype(jnp.bfloat16)
    d_value_b = d_value_sum.astype(jnp.bfloat16)
    d_projected = jnp.stack((d_query_b, d_key_b, d_value_b), axis=1).reshape(-1, 3 * local_width)
    d_qkv = product_tn(normed_b, d_projected).reshape(model_width, 3, local_width)
    d_q_bias = jnp.sum(d_query_b.astype(jnp.float32), axis=0)
    d_v_bias = jnp.sum(d_value_b.astype(jnp.float32), axis=0)
    normed_terms = product_nt(d_projected, qkv_flat)
    d_normed = lax.psum(normed_terms.astype(jnp.bfloat16), "tp").astype(jnp.float32)
    d_in_norm, d_gain_one, d_shift_one = norm1_pull(d_normed)
    input_grad = (d_middle + d_in_norm).astype(jnp.bfloat16)
    grad_qkv, grad_proj, grad_fc1, grad_fc2 = (
        lax.psum_scatter(d_qkv, ("shard", "ctx"), scatter_dimension=0, tiled=True),
        lax.psum_scatter(d_proj, ("shard", "ctx"), scatter_dimension=1, tiled=True),
        lax.psum_scatter(d_fc1, ("shard", "ctx"), scatter_dimension=0, tiled=True),
        lax.psum_scatter(d_fc2, ("shard", "ctx"), scatter_dimension=1, tiled=True),
    )
    small_sums = lax.psum(
        (
            d_q_bias,
            d_v_bias,
            d_proj_bias,
            d_gain_one,
            d_shift_one,
            d_gain_two,
            d_shift_two,
            d_fc1_bias,
            d_fc2_bias,
        ),
        ("shard", "ctx"),
    )
    return (
        out_rows[None],
        input_grad[None],
        grad_qkv,
        small_sums[0],
        small_sums[1],
        grad_proj,
        small_sums[2],
        small_sums[3],
        small_sums[4],
        small_sums[5],
        small_sums[6],
        grad_fc1,
        small_sums[7],
        grad_fc2,
        small_sums[8],
    )


def solution(mesh):
    in_specs = (
        P("shard", "ctx", None),
        P(("shard", "ctx"), None, "tp"),
        P("tp"),
        P("tp"),
        P("tp", ("shard", "ctx")),
        P(),
        P(),
        P(),
        P(),
        P(),
        P(("shard", "ctx"), "tp"),
        P("tp"),
        P("tp", ("shard", "ctx")),
        P(),
        P("shard", "ctx", None),
    )
    out_specs = (
        P("shard", "ctx", None),
        P("shard", "ctx", None),
        P(("shard", "ctx"), None, "tp"),
        P("tp"),
        P("tp"),
        P("tp", ("shard", "ctx")),
        P(),
        P(),
        P(),
        P(),
        P(),
        P(("shard", "ctx"), "tp"),
        P("tp"),
        P("tp", ("shard", "ctx")),
        P(),
    )
    return jax.shard_map(body, mesh=mesh, in_specs=in_specs, out_specs=out_specs, check_vma=False)
```

profile of v0, /device:TPU:0, one launch (start us, length us, event | category | flops | bytes accessed | tf_op | source)
XLA Modules:
  0.0 884.7 jit_solution(10069485723294902091)
XLA Ops:
  10.8 1.8 convert_reduce_fusion.1
  12.6 2.0 fusion.53
  14.7 32.2 %all_gather.25 = bf16[256,1024]{1,0:T(8,128)(2,1)} all-gather(bf16[256,128]{1,0:T(8,128)(2,1)S(1)} %copy-done.23), channel_id=1, replica_groups=mesh['shard'=4,'ctx'=2,'tp'=4] {'shard','ctx'}, dimensions={1}, use_global_device_ids=true | all-gather | bytes 589824 | tf_op jit(solution)/shard_map/all_gather | solution.py:70
  46.8 13.4 %all-gather.5.cloned.1.call-done = bf16[1024,3,256]{2,0,1:T(8,128)(2,1)} async-done(((bf16[128,3,256]{2,0,1:T(8,128)(2,1)}), bf16[1024,3,256]{2,0,1:T(8,128)(2,1)}) %all-gather.5.cloned.1.call-update) | async-done | bytes 1572880 | tf_op jit(solution)/shard_map/all_gather | solution.py:69
  60.2 1.7 copy.37
  62.0 1.7 fusion.78
  64.7 10.7 %all_gather.24 = bf16[1568,256]{1,0:T(8,128)(2,1)S(1)} all-gather(bf16[784,256]{1,0:T(8,128)(2,1)S(1)} %fusion.83), channel_id=1, replica_groups=mesh['shard'=4,'ctx'=2,'tp'=4] {'ctx'}, dimensions={0}, use_global_device_ids=true | all-gather | bytes 1204224 | tf_op jit(solution)/shard_map/all_gather | solution.py:111
  76.1 1.6 copy.43
  77.7 9.8 %all-gather = bf16[1568,1,256]{2,0,1:T(8,128)(2,1)S(1)} all-gather(bf16[784,1,256]{2,0,1:T(8,128)(2,1)S(1)} %slice.22), channel_id=2, replica_groups=mesh['shard'=4,'ctx'=2,'tp'=4] {'ctx'}, dimensions={0}, use_global_device_ids=true | all-gather | bytes 1204224 | tf_op jit(solution)/shard_map/all_gather | solution.py:110
  89.1 1.4 copy.38
  91.1 32.9 %while.26 = (s32[]{:T(128)}, bf16[4,784,64]{1,2,0:T(8,128)(2,1)S(1)}, f32[4,784]{1,0:T(4,128)S(1)}, bf16[4,784,64]{2,1,0:T(8,128)(2,1)S(1)}, bf16[4,1568,64]{2,1...) while((s32[]{:T(128)}, bf16[4,784,64]{1,2,0:T(8,128)(2,1)S(1)}, ...), condition=%wide.region_5.6_spmd, body=%wide.region_2.5_spmd.sunk | while | flops 325766912 | bytes 35996404 | solution.py:126
  92.1 2.3 copy-done
  95.5 3.8 fusion.135
  100.3 2.3 copy-done
  103.7 3.8 fusion.135
  108.5 2.3 copy-done
  111.9 3.8 fusion.135
  116.7 2.3 copy-done
  120.1 3.8 fusion.135
  124.0 3.7 fusion.98
  129.5 68.9 %all-reduce.6.cloned.1.call-done = f32[784,1024]{1,0:T(8,128)} async-done(((f32[784,1024]{1,0:T(8,128)}), f32[784,1024]{1,0:T(8,128)}) %all-reduce.6.cloned.1.call-update) | async-done | bytes 3211280 | tf_op jit(solution)/shard_map/psum | solution.py:129
  198.4 2.9 fusion.96
  201.7 48.4 %all-gather.7.cloned.1.call-done = bf16[1024,1024]{1,0:T(8,128)(2,1)} async-done(((bf16[128,1024]{1,0:T(8,128)(2,1)}), bf16[1024,1024]{1,0:T(8,128)(2,1)}) %all-gather.7.cloned.1.call-update) | async-done | bytes 2097168 | tf_op jit(solution)/shard_map/all_gather | solution.py:71
  250.1 12.5 %multiply_convert_fusion.1 = (bf16[784,1024]{1,0:T(8,128)(2,1)}, f32[784,1024]{1,0:T(8,128)}, f32[784,1024]{1,0:T(8,128)}) fusion(f32[1024]{0:T(1024)S(1)} %convert_element_type.176, bf16[1024,1024]{1,0:T(8,128)(2,1)} %all-gather.7.cloned.1.call-done, f32[784,1024]{1,0:T(8,128)S(1)} %get-tuple-element.172, f32[1024]{0:T(1024)S(1)} %convert_element_type.174, ...), kind=kOutput, calls=%fused_computation.87 | convolution fusion | flops 1701167104 | bytes 13355136 | tf_op jit(solution)/shard_map/dot_general | solution.py:32
  262.7 39.2 %all-gather.9.cloned.1.call-done = bf16[1024,1024]{1,0:T(8,128)(2,1)} async-done(((bf16[1024,128]{1,0:T(8,128)(2,1)}), bf16[1024,1024]{1,0:T(8,128)(2,1)}) %all-gather.9.cloned.1.call-update) | async-done | bytes 2097168 | tf_op jit(solution)/shard_map/all_gather | solution.py:72
  301.8 7.0 convert_reduce_fusion.3
  310.0 3.6 fusion.99
  313.9 67.6 %all-reduce.8.cloned.1.call-done = f32[784,1024]{1,0:T(8,128)} async-done(((f32[784,1024]{1,0:T(8,128)}), f32[784,1024]{1,0:T(8,128)}) %all-reduce.8.cloned.1.call-update) | async-done | bytes 3211280 | tf_op jit(solution)/shard_map/psum | solution.py:155
  381.4 3.1 multiply_reduce_fusion.2
  390.0 2.0 copy.44
  392.8 39.0 %while.27 = (s32[]{:T(128)}, bf16[4,784,64]{1,2,0:T(8,128)(2,1)}, bf16[4,1568,64]{1,2,0:T(8,128)(2,1)}, bf16[4,1568,64]{1,2,0:T(8,128)(2,1)}, bf16[4,784,64]{2,1...) while((s32[]{:T(128)}, bf16[4,784,64]{1,2,0:T(8,128)(2,1)}, ...), condition=%wide.region_15.16_spmd, body=%wide.region_13.15_spmd.sunk | while | flops 796743936 | bytes 54870544 | solution.py:175
  392.8 2.1 fusion.144
  395.0 1.7 multiply_reduce_fusion.8
  400.4 2.1 fusion.147
  402.6 2.1 fusion.144
  404.8 1.7 multiply_reduce_fusion.8
  410.2 2.1 fusion.147
  412.3 2.1 fusion.144
  414.5 1.7 multiply_reduce_fusion.8
  420.0 2.1 fusion.147
  422.1 2.1 fusion.144
  424.3 1.7 multiply_reduce_fusion.8
  429.7 2.1 fusion.147
  431.9 2.1 copy.49
  434.1 2.2 copy.50
  436.3 5.1 convolution_convert_fusion
  441.4 2.0 copy.51
  443.3 8.6 reduce-scatter.7.cloned.1.call-done
  451.9 20.0 %reduce-scatter.9.cloned.1.call-done = bf16[784,256]{1,0:T(8,128)(2,1)} async-done(((bf16[1568,256]{1,0:T(8,128)(2,1)}), bf16[784,256]{1,0:T(8,128)(2,1)}) %reduce-scatter.9.cloned.1.call-update) | async-done | bytes 401424 | tf_op jit(solution)/shard_map/reduce_scatter | solution.py:182
  471.9 4.4 bitcast_convert_fusion
  476.4 3.3 fusion.100
  480.0 5.9 fusion.91
  486.0 6.3 fusion.71
  493.0 5.7 fusion.80
  501.1 45.1 %all-reduce.10.cloned.1.call-done = (bf16[784,1024]{1,0:T(8,128)(2,1)}, bf16[784,1024]{1,0:T(8,128)(2,1)}) async-done(((bf16[784,1024]{1,0:T(8,128)(2,1)}, bf16[784,1024]{1,0:T(8,128)(2,1)}), (bf16[784,1024]{1,0:T(8,128)(2,1)}, bf16[784,1024]{1,0:T(8,128)(2,1)})) %all-reduce.10.cloned.1.call-update) | async-done | bytes 3211280 | tf_op jit(solution)/shard_map/psum | solution.py:137
  546.2 3.1 convert_reduce_fusion
  549.4 1.9 fusion.61
  551.3 3.8 convert_reduce_fusion.2
  555.1 37.9 %all-reduce = (f32[256]{0:T(256)}, f32[256]{0:T(256)}, f32[1024]{0:T(1024)}, f32[1024]{0:T(1024)}, f32[1024]{0:T(1024)}, /*index=5*/f32[1024]{0:T(1024)}, f32[1024]{0:T(1024)}, f32[1024]{0:T(1024)}, f32[1024]{0:T(1024)}) all-reduce(f32[256]{0:T(256)S(1)} %reduce_sum.186, ...), channel_id=1, replica_groups=mesh['shard'=4,'ctx'=2,'tp'=4] {'shard','ctx'}, use_global_device_ids=true, to_apply=%region_23.24 | all-reduce | flops 7680 | bytes 61440 | tf_op jit(solution)/shard_map/psum | solution.py:203
  592.9 3.2 fusion.69
  596.1 18.6 %reduce-scatter.13.cloned.1.call-done = f32[256,128]{1,0:T(8,128)} async-done(((f32[256,1024]{1,0:T(8,128)}), f32[256,128]{1,0:T(8,128)}) %reduce-scatter.13.cloned.1.call-update) | async-done | bytes 131088 | tf_op jit(solution)/shard_map/reduce_scatter | solution.py:199
  614.7 90.9 %reduce-scatter.15.cloned.1.call-done = f32[128,1024]{1,0:T(8,128)} async-done(((f32[1024,1024]{1,0:T(8,128)}), f32[128,1024]{1,0:T(8,128)}) %reduce-scatter.15.cloned.1.call-update) | async-done | bytes 524304 | tf_op jit(solution)/shard_map/reduce_scatter | solution.py:200
  705.6 93.0 %reduce-scatter.17.cloned.1.call-done = f32[1024,128]{1,0:T(8,128)} async-done(((f32[1024,1024]{1,0:T(8,128)}), f32[1024,128]{1,0:T(8,128)}) %reduce-scatter.17.cloned.1.call-update) | async-done | bytes 524304 | tf_op jit(solution)/shard_map/reduce_scatter | solution.py:201
  798.6 78.8 %reduce-scatter.11.cloned.1.call-done = f32[128,3,256]{2,0,1:T(8,128)} async-done(((f32[1024,3,256]{2,0,1:T(8,128)}), f32[128,3,256]{2,0,1:T(8,128)}) %reduce-scatter.11.cloned.1.call-update) | async-done | bytes 393232 | tf_op jit(solution)/shard_map/reduce_scatter | solution.py:198
  (209 shorter events, 43.9 us)
Async XLA Ops:
  7.2 7.5 copy-start.23
  7.2 53.1 %all-gather.5.cloned.1.call-start = ((), (), s32[]{:S(2)}) async-start(), calls=%async_computation.6 | async-start | bytes 1769472 | tf_op jit(solution)/shard_map/all_gather | solution.py:69
  7.9 190.4 %all-reduce.6.cloned.1.call-start = ((), (), s32[]{:S(2)}) async-start(), calls=%async_computation.7 | async-start | bytes 6422528 | tf_op jit(solution)/shard_map/psum | solution.py:129
  8.7 53.3 %copy-start.21 = (f32[1024]{0:T(1024)}, f32[1024]{0:T(1024)S(1)}, u32[]{:S(2)}) copy-start(f32[1024]{0:T(1024)S(1)} %convert_element_type.161) | copy-start | bytes 12292
  9.4 52.6 %copy-start.28 = (f32[1024]{0:T(1024)}, f32[1024]{0:T(1024)S(1)}, u32[]{:S(2)}) copy-start(f32[1024]{0:T(1024)S(1)} %convert_element_type.162) | copy-start | bytes 12292
  10.8 51.2 %copy-start.1 = (bf16[1,784,1024]{2,1,0:T(8,128)(2,1)S(1)}, bf16[1,784,1024]{2,1,0:T(8,128)(2,1)}, u32[]{:S(2)}) copy-start(bf16[1,784,1024]{2,1,0:T(8,128)(2,1)} %param.19) | copy-start | bytes 4816900
  12.6 51.1 %copy-start.19 = (f32[784]{0:T(1024)}, f32[784]{0:T(1024)S(1)}, u32[]{:S(2)}) copy-start(f32[784]{0:T(1024)S(1)} %broadcast_multiply_fusion.1) | copy-start | bytes 9412
  14.6 49.0 %copy-start.26 = (f32[784]{0:T(1024)}, f32[784]{0:T(1024)S(1)}, u32[]{:S(2)}) copy-start(f32[784]{0:T(1024)S(1)} %fusion.53) | copy-start | bytes 9412
  14.6 49.0 %copy-start.24 = (f32[784]{0:T(1024)}, f32[784]{0:T(1024)S(1)}, u32[]{:S(2)}) copy-start(f32[784]{0:T(1024)S(1)} %fusion.85) | copy-start | bytes 9412
  92.0 2.3 copy-start
  100.3 2.3 copy-start
  108.5 2.3 copy-start
  116.7 2.3 copy-start
  124.0 3.8 copy-start.3
  124.0 3.8 copy-start.7
  124.0 3.8 copy-start.13
  127.8 1.6 copy-start.30
  127.8 1.6 copy-start.31
  127.8 1.6 copy-start.32
  127.8 1.6 copy-start.33
  127.8 122.3 %all-gather.7.cloned.1.call-start = ((), (), s32[]{:S(2)}) async-start(), calls=%async_computation.8 | async-start | bytes 2359296 | tf_op jit(solution)/shard_map/all_gather | solution.py:71
  128.6 173.3 %all-gather.9.cloned.1.call-start = ((), (), s32[]{:S(2)}) async-start(), calls=%async_computation.9 | async-start | bytes 2359296 | tf_op jit(solution)/shard_map/all_gather | solution.py:72
  129.2 252.3 %all-reduce.8.cloned.1.call-start = ((), (), s32[]{:S(2)}) async-start(), calls=%async_computation.10 | async-start | bytes 6422528 | tf_op jit(solution)/shard_map/psum | solution.py:155
  301.8 8.2 copy-start.35
  308.8 1.2 copy-start.36
  313.6 138.3 %reduce-scatter.7.cloned.1.call-start = ((), (), s32[]{:S(2)}) async-start(), calls=%async_computation.11 | async-start | bytes 1204224 | tf_op jit(solution)/shard_map/reduce_scatter | solution.py:179
  381.4 3.2 copy-start.10
  384.6 1.4 copy-start.11
  385.7 1.8 copy-start.5
  386.0 2.6 copy-start.16
  387.5 1.2 copy-start.12
  392.8 2.2 copy-start.4
  392.8 2.2 copy-start.8
  396.7 1.2 copy-start.17
  397.6 1.1 copy-start.14
  398.5 1.9 copy-start.18
  402.6 2.2 copy-start.4
  402.6 2.2 copy-start.8
  406.4 1.2 copy-start.17
  407.3 1.1 copy-start.14
  408.3 1.9 copy-start.18
  409.4 0.8 copy-start.15
  412.3 2.2 copy-start.4
  412.3 2.2 copy-start.8
  416.2 1.2 copy-start.17
  417.1 1.1 copy-start.14
  418.0 1.9 copy-start.18
  422.1 2.2 copy-start.4
  422.1 2.2 copy-start.8
  426.0 1.2 copy-start.17
  426.9 1.1 copy-start.14
  427.8 2.0 copy-start.18
  428.9 0.8 copy-start.15
  434.0 37.9 %reduce-scatter.9.cloned.1.call-start = ((), (), s32[]{:S(2)}) async-start(), calls=%async_computation.12 | async-start | bytes 1204224 | tf_op jit(solution)/shard_map/reduce_scatter | solution.py:182
  436.3 109.9 %all-reduce.10.cloned.1.call-start = ((), (), s32[]{:S(2)}) async-start(), calls=%async_computation.17 | async-start | bytes 6422528 | tf_op jit(solution)/shard_map/psum | solution.py:137
  476.3 138.4 %reduce-scatter.13.cloned.1.call-start = ((), (), s32[]{:S(2)}) async-start(), calls=%async_computation.14 | async-start | bytes 1179648 | tf_op jit(solution)/shard_map/reduce_scatter | solution.py:199
  479.7 226.0 %reduce-scatter.15.cloned.1.call-start = ((), (), s32[]{:S(2)}) async-start(), calls=%async_computation.15 | async-start | bytes 4718592 | tf_op jit(solution)/shard_map/reduce_scatter | solution.py:200
  485.9 312.7 %reduce-scatter.17.cloned.1.call-start = ((), (), s32[]{:S(2)}) async-start(), calls=%async_computation.16 | async-start | bytes 4718592 | tf_op jit(solution)/shard_map/reduce_scatter | solution.py:201
  492.3 6.4 copy-start.34
  492.3 385.1 %reduce-scatter.11.cloned.1.call-start = ((), (), s32[]{:S(2)}) async-start(), calls=%async_computation.13 | async-start | bytes 3538944 | tf_op jit(solution)/shard_map/reduce_scatter | solution.py:198
  498.7 50.7 %copy-start.27 = (f32[784]{0:T(1024)S(1)}, f32[784]{0:T(1024)}, u32[]{:S(2)}) copy-start(f32[784]{0:T(1024)} %copy-done.26) | copy-start | bytes 9412
  546.2 3.1 copy-start.2
  546.2 3.2 copy-start.9
  546.2 5.1 copy-start.6
  (6 other events, 4.4 us)
Sparse Core Ops, SparseCore 0:
  10.2 49.9 all-gather.4
  128.0 70.3 all-reduce.5
  200.7 49.3 all-gather.6
  252.2 49.5 all-gather.8
  313.7 67.6 all-reduce.7
  434.2 17.6 reduce-scatter.6
  454.2 17.6 reduce-scatter.8
  476.4 69.7 all-reduce.9
  550.6 64.0 reduce-scatter.12
  618.7 86.8 reduce-scatter.14
  710.3 88.2 reduce-scatter.16
  802.6 74.7 reduce-scatter.10
where the time goes:
time: 892 us; the launch traced here: 885 us
  waiting for transfers between devices  594 us (67%)
  matrix products  110 us (12%)
  blocking collectives  90.5 us (10%)
  local copies, waits for them, and re-layouts  36.8 us (4%)
  other arithmetic  36.1 us (4%)
  between operations  15.1 us (2%)
    reduce_scatter x1, waiting for transfers between devices, body(): lax.psum_scatter(d_fc2, ('shard', 'ctx'), scatter_dimension=1, tiled=True)  93 us
    reduce_scatter x1, waiting for transfers between devices, body(): lax.psum_scatter(d_fc1, ('shard', 'ctx'), scatter_dimension=0, tiled=True)  90.9 us
    reduce_scatter x1, waiting for transfers between devices, body(): lax.psum_scatter(d_qkv, ('shard', 'ctx'), scatter_dimension=0, tiled=True)  78.8 us
    psum x1, waiting for transfers between devices, body(): middle = inputs + lax.psum(attn_terms, 'tp') + proj_bias_f  68.9 us
    psum x1, waiting for transfers between devices, body(): d_second = lax.psum(second_terms, 'tp')  67.6 us
    all_gather x1, waiting for transfers between devices, body(): lax.all_gather(owned[2], ('shard', 'ctx'), axis=0, tiled=True)  48.4 us
    psum x1, waiting for transfers between devices, body(): lax.psum(mlp_terms.astype(jnp.bfloat16), 'tp').astype(jnp.float32)  45.1 us
    dot_general x12, matrix products, product(): return jnp.dot(left, right, preferred_element_type=jnp.float32)  42.3 us
  transfers between devices with their start and end apart: 12, of which 12 were waited for; matrix products, arithmetic and copies ran while one was open for 8% of the time, Pallas kernels for 0%

commit v1 on v0

v1 whole, which is shorter than its diff:
```python
import functools

import jax
import jax.numpy as jnp
from jax import lax
from jax.experimental import pallas as pl
from jax.experimental.pallas import tpu as pltpu
from jax.sharding import PartitionSpec as P

HD = 64
HEADS = 4
WIDTH = HEADS * HD
QTILE = 112
KTILE = 112

norm_eps = 1e-06
bf16, f32 = jnp.bfloat16, jnp.float32
VMEM_LIMIT = 32 * 1024 * 1024

CTX_PAIRS = [(0, 1), (1, 0)]
CORE_PAIRS = [(0, 1), (1, 0), (2, 3), (3, 2)]
FAR_PAIRS = [(0, 2), (2, 0), (1, 3), (3, 1)]


def params(**more):
    return pltpu.CompilerParams(vmem_limit_bytes=VMEM_LIMIT, **more)


def norm_rows(values, gain, shift):
    row_mean = jnp.mean(values, axis=-1, keepdims=True)
    centered = values - row_mean
    variance = jnp.mean(centered * centered, axis=-1, keepdims=True)
    return centered * lax.rsqrt(variance + norm_eps) * gain + shift


def dot_nn(left, right):
    return jnp.dot(left, right, preferred_element_type=f32)


def dot_tn(left, right):
    return lax.dot_general(left, right, (((0,), (0,)), ((), ())), preferred_element_type=f32)


def dot_nt(left, right):
    return lax.dot_general(left, right, (((1,), (1,)), ((), ())), preferred_element_type=f32)


def ctx_swap(value):
    return lax.ppermute(value, "ctx", CTX_PAIRS)


def ring_gather(piece, count):
    down = [(i, (i - 1) % count) for i in range(count)]
    pieces = [piece]
    for _ in range(count - 1):
        pieces.append(lax.ppermute(pieces[-1], "shard", down))
    return pieces


def ring_scatter(kept, count):
    up = [(i, (i + 1) % count) for i in range(count)]
    me = lax.axis_index("shard")

    def block(step):
        return lax.dynamic_index_in_dim(kept, (me + step) % count, 0, keepdims=False)

    if count == 1:
        return block(0).astype(f32)
    total = block(count - 1).astype(bf16)
    for step in range(count - 2, -1, -1):
        arrived = lax.ppermute(total, "shard", up)
        total = block(step).astype(f32) + arrived.astype(f32)
        if step:
            total = total.astype(bf16)
    return total


def assemble_kernel(count, rows, *refs):
    pieces, out = refs[: 2 * count], refs[2 * count]
    shard, ctx = lax.axis_index("shard"), lax.axis_index("ctx")
    for side in range(2):
        for step in range(count):
            owner = lax.rem(shard + step, count) * 2 + (ctx + side) % 2
            out[pl.ds(pl.multiple_of(owner * rows, rows), rows), :] = pieces[side * count + step][...]


def assemble(own, other):
    count = len(own)
    rows, columns = own[0].shape
    return pl.pallas_call(
        functools.partial(assemble_kernel, count, rows),
        out_shape=jax.ShapeDtypeStruct((2 * count * rows, columns), bf16),
        compiler_params=params(),
        name="assemble",
    )(*own, *other)


def tp_sum(terms):
    core = lax.axis_index("tp") % 2
    half = terms.shape[0] // 2
    keep = lax.dynamic_slice_in_dim(terms, core * half, half, 0)
    send = lax.dynamic_slice_in_dim(terms, (1 - core) * half, half, 0)
    near = (keep.astype(f32) + lax.ppermute(send, "tp", CORE_PAIRS).astype(f32)).astype(bf16)
    near = lax.optimization_barrier(near)
    total = (near.astype(f32) + lax.ppermute(near, "tp", FAR_PAIRS).astype(f32)).astype(bf16)
    total = lax.optimization_barrier(total)
    other = lax.ppermute(total, "tp", CORE_PAIRS)
    return jnp.where(core == 0, jnp.concatenate([total, other]), jnp.concatenate([other, total]))


def small_sum(vector, count):
    vector = vector + ctx_swap(vector)
    step = 1
    while step < count:
        vector = vector + lax.ppermute(vector, "shard", [(i, i ^ step) for i in range(count)])
        step *= 2
    return vector


def head_mask(shape, head):
    lane = lax.broadcasted_iota(jnp.int32, shape, len(shape) - 1)
    return (lane >= head * HD) & (lane < (head + 1) * HD)


def fwd_near_kernel(q_ref, kv_ref, o_ref, m_ref, l_ref):
    q = q_ref[...]
    keys, values = kv_ref[:, :WIDTH], kv_ref[:, WIDTH:]
    rows = q.shape[0]
    o = jnp.zeros((rows, WIDTH), f32)
    m = jnp.zeros((rows, WIDTH), f32)
    total = jnp.zeros((rows, WIDTH), f32)
    for head in range(HEADS):
        mask = head_mask((rows, WIDTH), head)
        scores = dot_nt(jnp.where(mask, q, jnp.zeros_like(q)), keys)
        top = jnp.max(scores, axis=-1, keepdims=True)
        weights = jnp.exp(scores - top)
        row_sum = jnp.sum(weights, axis=-1, keepdims=True)
        mixed = dot_nn(weights.astype(bf16), values)
        o = jnp.where(mask, mixed, o)
        m = jnp.where(mask, top, m)
        total = jnp.where(mask, row_sum, total)
    o_ref[...] = o
    m_ref[...] = m
    l_ref[...] = total


def fwd_far_kernel(q_ref, kv_ref, o_ref, m_ref, l_ref, mix_ref, lse_ref):
    q = q_ref[...]
    keys, values = kv_ref[:, :WIDTH], kv_ref[:, WIDTH:]
    rows = q.shape[0]
    o, m, total = o_ref[...], m_ref[...], l_ref[...]
    o_out = jnp.zeros((rows, WIDTH), f32)
    lse = jnp.zeros((rows, 128), f32)
    lane = lax.broadcasted_iota(jnp.int32, (rows, 128), 1)
    for head in range(HEADS):
        mask = head_mask((rows, WIDTH), head)
        scores = dot_nt(jnp.where(mask, q, jnp.zeros_like(q)), keys)
        before = m[:, head * HD : head * HD + 1]
        top = jnp.maximum(jnp.max(scores, axis=-1, keepdims=True), before)
        weights = jnp.exp(scores - top)
        carry = jnp.exp(before - top)
        row_sum = jnp.sum(weights, axis=-1, keepdims=True) + carry * total[:, head * HD : head * HD + 1]
        mixed = dot_nn(weights.astype(bf16), values) + carry * o
        o_out = jnp.where(mask, mixed / row_sum, o_out)
        lse = jnp.where(lane == head, top + jnp.log(row_sum), lse)
    mix_ref[...] = o_out.astype(bf16)
    lse_ref[...] = lse


def attention_near(q, kv):
    rows, keys = q.shape[0], kv.shape[0]
    tile = pl.BlockSpec((QTILE, WIDTH), lambda i: (i, 0))
    return pl.pallas_call(
        fwd_near_kernel,
        grid=(rows // QTILE,),
        out_shape=[jax.ShapeDtypeStruct((rows, WIDTH), f32)] * 3,
        in_specs=[tile, pl.BlockSpec((keys, 2 * WIDTH), lambda i: (0, 0))],
        out_specs=[tile] * 3,
        compiler_params=params(),
        cost_estimate=pl.CostEstimate(flops=16 * rows * keys * WIDTH, bytes_accessed=1 << 22, transcendentals=0),
        name="attention_near",
    )(q, kv)


def attention_far(q, kv, o, m, total):
    rows, keys = q.shape[0], kv.shape[0]
    tile = pl.BlockSpec((QTILE, WIDTH), lambda i: (i, 0))
    return pl.pallas_call(
        fwd_far_kernel,
        grid=(rows // QTILE,),
        out_shape=[jax.ShapeDtypeStruct((rows, WIDTH), bf16), jax.ShapeDtypeStruct((rows, 128), f32)],
        in_specs=[tile, pl.BlockSpec((keys, 2 * WIDTH), lambda i: (0, 0)), tile, tile, tile],
        out_specs=[tile, pl.BlockSpec((QTILE, 128), lambda i: (i, 0))],
        compiler_params=params(),
        cost_estimate=pl.CostEstimate(flops=16 * rows * keys * WIDTH, bytes_accessed=1 << 22, transcendentals=0),
        name="attention_far",
    )(q, kv, o, m, total)


def bwd_kernel(k_ref, v_ref, q_ref, do_ref, lse_ref, delta_ref, dkv_ref, dq_ref):
    @pl.when(pl.program_id(0) == 0)
    def _():
        dq_ref[...] = jnp.zeros_like(dq_ref)

    q, d_out = q_ref[...], do_ref[...]
    keys, values = k_ref[...], v_ref[...]
    rows = keys.shape[0]
    dk = jnp.zeros((rows, WIDTH), f32)
    dv = jnp.zeros((rows, WIDTH), f32)
    dq = dq_ref[...]
    for head in range(HEADS):
        mask = head_mask((rows, WIDTH), head)
        head_k = jnp.where(mask, keys, jnp.zeros_like(keys))
        head_v = jnp.where(mask, values, jnp.zeros_like(values))
        probs = jnp.exp(dot_nt(head_k, q) - lse_ref[head : head + 1, :])
        d_probs = dot_nt(head_v, d_out)
        dv = jnp.where(mask, dot_nn(probs.astype(bf16), d_out), dv)
        d_scores = (probs * (d_probs - delta_ref[head : head + 1, :])).astype(bf16)
        dk = jnp.where(mask, dot_nn(d_scores, q), dk)
        dq = dq + dot_tn(d_scores, head_k)
    dkv_ref[:, :WIDTH] = dk
    dkv_ref[:, WIDTH:] = dv
    dq_ref[...] = dq


def attention_back(q, kv, d_out, lse, delta):
    rows, keys = q.shape[0], kv.shape[0]
    whole = pl.BlockSpec((rows, WIDTH), lambda i: (0, 0))
    line = pl.BlockSpec(lse.shape, lambda i: (0, 0))
    return pl.pallas_call(
        bwd_kernel,
        grid=(keys // KTILE,),
        out_shape=[jax.ShapeDtypeStruct((keys, 2 * WIDTH), f32), jax.ShapeDtypeStruct((rows, WIDTH), f32)],
        in_specs=[
            pl.BlockSpec((KTILE, WIDTH), lambda i: (i, 0)),
            pl.BlockSpec((KTILE, WIDTH), lambda i: (i, 1)),
            whole,
            whole,
            line,
            line,
        ],
        out_specs=[pl.BlockSpec((KTILE, 2 * WIDTH), lambda i: (i, 0)), whole],
        compiler_params=params(),
        cost_estimate=pl.CostEstimate(flops=40 * rows * keys * WIDTH, bytes_accessed=1 << 22, transcendentals=0),
        name="attention_back",
    )(kv, kv, q, d_out, lse, delta)


def layer(
    count,
    video_tokens,
    qkv_weight,
    q_bias,
    v_bias,
    proj_weight,
    proj_bias,
    norm1_gain,
    norm1_shift,
    norm2_gain,
    norm2_shift,
    fc1_weight,
    fc1_bias,
    fc2_weight,
    fc2_bias,
    out_grad,
):
    score_scale = HD ** (-0.5)
    inputs = video_tokens[0].astype(f32)
    ctx = lax.axis_index("ctx")
    (q_bias_f, v_bias_f, proj_bias_f, gain_one, shift_one, gain_two, shift_two, fc1_bias_f, fc2_bias_f) = (
        param.astype(f32)
        for param in (q_bias, v_bias, proj_bias, norm1_gain, norm1_shift, norm2_gain, norm2_shift, fc1_bias, fc2_bias)
    )
    piece_a = jnp.concatenate([qkv_weight[:, 0], qkv_weight[:, 1], qkv_weight[:, 2], proj_weight.T], axis=1)
    own_a = ring_gather(piece_a, count)
    other_a = [ctx_swap(piece) for piece in own_a]
    piece_1, piece_2, _ = lax.optimization_barrier((fc1_weight, fc2_weight.T, own_a[-1]))
    own_1 = ring_gather(piece_1, count)
    own_2 = ring_gather(piece_2, count)
    weight_a = assemble(own_a, other_a)
    qkv_w, proj_t = weight_a[:, : 3 * WIDTH], weight_a[:, 3 * WIDTH :]

    normed, norm1_pull = jax.vjp(norm_rows, inputs, gain_one, shift_one)
    normed_b = normed.astype(bf16)
    projected = dot_nn(normed_b, qkv_w)
    queries = ((projected[:, :WIDTH] + q_bias_f).astype(bf16).astype(f32) * score_scale).astype(bf16)
    kv = jnp.concatenate(
        [projected[:, WIDTH : 2 * WIDTH].astype(bf16), (projected[:, 2 * WIDTH :] + v_bias_f).astype(bf16)], axis=1
    )
    kv_far = ctx_swap(kv)
    partial = attention_near(queries, kv)
    own_1, own_2, kv_far = lax.optimization_barrier((own_1, own_2, kv_far))
    other_1 = [ctx_swap(piece) for piece in own_1]
    other_2 = [ctx_swap(piece) for piece in own_2]
    mixture_b, lse = attention_far(queries, kv_far, *partial)
    attn_sum = tp_sum(dot_nt(mixture_b, proj_t).astype(bf16))
    weight_1 = assemble(own_1, other_1)
    weight_2 = assemble(own_2, other_2)

    middle = inputs + attn_sum.astype(f32) + proj_bias_f
    second, norm2_pull = jax.vjp(norm_rows, middle, gain_two, shift_two)
    second_b = second.astype(bf16)
    pre_act = dot_nn(second_b, weight_1) + fc1_bias_f
    hidden_f, gelu_pull = jax.vjp(lambda v: jax.nn.gelu(v, approximate=False), pre_act)
    hidden_b = hidden_f.astype(bf16)
    grad_b = out_grad[0]
    grad_f = grad_b.astype(f32)
    d_hidden = dot_nn(grad_b, weight_2)
    d_pre_b = gelu_pull(d_hidden)[0].astype(bf16)
    d_second = tp_sum(dot_nt(d_pre_b, weight_1).astype(bf16)).astype(f32)
    mlp_sum = tp_sum(dot_nt(hidden_b, weight_2).astype(bf16))
    out_rows = (middle + mlp_sum.astype(f32) + fc2_bias_f).astype(bf16)

    def scatter(grads):
        width, columns = grads.shape
        rows = width // (2 * count)
        split = grads.reshape(count, 2, rows, columns)
        keep = lax.dynamic_index_in_dim(split, ctx, 1, keepdims=False)
        send = lax.dynamic_index_in_dim(split, 1 - ctx, 1, keepdims=False).astype(bf16)
        kept = keep.astype(f32) + ctx_swap(send).astype(f32)
        return ring_scatter(kept, count)

    d_fc1 = dot_tn(second_b, d_pre_b)
    d_fc2_t = dot_tn(grad_b, hidden_b)
    grad_fc1 = scatter(d_fc1)
    grad_fc2 = scatter(d_fc2_t).T
    d_fc1_bias = jnp.sum(d_pre_b.astype(f32), axis=0)
    d_fc2_bias = jnp.sum(grad_f, axis=0)

    d_mid_norm, d_gain_two, d_shift_two = norm2_pull(d_second)
    d_middle = grad_f + d_mid_norm
    d_middle_b = d_middle.astype(bf16)
    d_proj_t = dot_tn(d_middle_b, mixture_b)
    d_proj_bias = jnp.sum(d_middle_b.astype(f32), axis=0)
    d_mixture_b = dot_nn(d_middle_b, proj_t).astype(bf16)
    early = small_sum(jnp.concatenate([d_fc1_bias, d_fc2_bias, d_gain_two, d_shift_two, d_proj_bias]), count)

    rows = d_mixture_b.shape[0]
    delta = jnp.sum((d_mixture_b.astype(f32) * mixture_b.astype(f32)).reshape(rows, HEADS, HD), axis=-1)
    delta_t, lse_t = delta.T, lse[:, :HEADS].T
    dkv_away, dq_away = attention_back(queries, kv_far, d_mixture_b, lse_t, delta_t)
    dkv_back = ctx_swap(dkv_away.astype(bf16))
    dkv_here, dq_here = attention_back(queries, kv, d_mixture_b, lse_t, delta_t)
    d_query_b = ((dq_away + dq_here) * score_scale).astype(bf16)
    d_kv_b = (dkv_here + dkv_back.astype(f32)).astype(bf16)
    d_projected = jnp.concatenate([d_query_b, d_kv_b], axis=1)
    d_q_bias = jnp.sum(d_query_b.astype(f32), axis=0)
    d_v_bias = jnp.sum(d_kv_b[:, WIDTH:].astype(f32), axis=0)
    d_normed = tp_sum(dot_nt(d_projected, qkv_w).astype(bf16)).astype(f32)
    d_qkv = dot_tn(normed_b, d_projected)
    grad_a = scatter(jnp.concatenate([d_qkv, d_proj_t], axis=1))
    grad_qkv = grad_a[:, : 3 * WIDTH].reshape(-1, 3, WIDTH)
    grad_proj = grad_a[:, 3 * WIDTH :].T
    d_in_norm, d_gain_one, d_shift_one = norm1_pull(d_normed)
    input_grad = (d_middle + d_in_norm).astype(bf16)
    late = small_sum(jnp.concatenate([d_q_bias, d_v_bias, d_gain_one, d_shift_one]), count)
    width, hidden = inputs.shape[1], fc1_bias.shape[0]
    g_fc1_bias, g_fc2_bias, g_gain_two, g_shift_two, g_proj_bias = (
        early[:hidden],
        *(early[hidden + i * width : hidden + (i + 1) * width] for i in range(4)),
    )
    return (
        out_rows[None],
        input_grad[None],
        grad_qkv,
        late[:WIDTH],
        late[WIDTH : 2 * WIDTH],
        grad_proj,
        g_proj_bias,
        late[2 * WIDTH : 2 * WIDTH + width],
        late[2 * WIDTH + width :],
        g_gain_two,
        g_shift_two,
        grad_fc1,
        g_fc1_bias,
        grad_fc2,
        g_fc2_bias,
    )


def solution(mesh):
    split = ("shard", "ctx")
    tokens, rows, columns = P("shard", "ctx", None), P(split, "tp"), P("tp", split)
    stack = P(split, None, "tp")
    own, copied = P("tp"), P()
    in_specs = (
        tokens,
        stack,
        own,
        own,
        columns,
        copied,
        copied,
        copied,
        copied,
        copied,
        rows,
        own,
        columns,
        copied,
        tokens,
    )
    out_specs = (
        tokens,
        tokens,
        stack,
        own,
        own,
        columns,
        copied,
        copied,
        copied,
        copied,
        copied,
        rows,
        own,
        columns,
        copied,
    )
    return jax.shard_map(
        functools.partial(layer, mesh.shape["shard"]),
        mesh=mesh,
        in_specs=in_specs,
        out_specs=out_specs,
        check_vma=False,
    )
```

time: 892 us -> 462 us (0.52)
  waiting for transfers between devices: 594 us -> 180 us
  blocking collectives: 90.5 us -> 0 us
  matrix products: 110 us -> 34.8 us
  Pallas kernels: 0 us -> 69.2 us
  starting transfers between devices: 1.12 us -> 48.9 us
  other arithmetic: 36.1 us -> 66.1 us
  local copies, waits for them, and re-layouts: 36.8 us -> 55.4 us
  between operations: 15.1 us -> 2.44 us
    reduce_scatter x6 -> x0, waiting for transfers between devices: 310 us -> none  [the longest x1 93 us: body(): lax.psum_scatter(d_fc2, ('shard', 'ctx'), scatter_dimension=1, tiled=True)]
    psum x3 -> x0, waiting for transfers between devices: 182 us -> none  [the longest x1 68.9 us: body(): middle = inputs + lax.psum(attn_terms, 'tp') + proj_bias_f]
    ppermute x0 -> x53, waiting for transfers between devices: none -> 180 us  [the longest x19 63.5 us: ctx_swap(): return lax.ppermute(value, 'ctx', CTX_PAIRS)]
    all_gather x3 -> x0, waiting for transfers between devices: 101 us -> none  [the longest x1 48.4 us: body(): lax.all_gather(owned[2], ('shard', 'ctx'), axis=0, tiled=True)]
    dot_general x40 -> x12, matrix products: 110 us -> 34.8 us  [the longest x4 19.1 us: dot_nn(): return jnp.dot(left, right, preferred_element_type=f32)]
    pallas_call x0 -> x7, Pallas kernels: none -> 69.2 us  [the longest x2 35.2 us: attention_back(): pl.pallas_call(bwd_kernel, grid=(keys // KTILE,), out_shape=[jax.ShapeDty...]
    all_gather x3 -> x0, blocking collectives: 52.7 us -> none  [the longest x1 32.2 us: body(): lax.all_gather(owned[1], ('shard', 'ctx'), axis=1, tiled=True)]
    ppermute x0 -> x53, starting transfers between devices: none -> 48.9 us  [the longest x9 22.7 us: ring_gather(): pieces.append(lax.ppermute(pieces[-1], 'shard', down))]
  transfers between devices with their start and end apart: 12 -> 53, of which waited for: 12 -> 32; matrix products, arithmetic and copies ran while one was open for 8% -> 23% of each run, Pallas kernels for 0% -> 11%
where the time goes in v1:
time: 462 us; the launch traced here: 457 us
  waiting for transfers between devices  180 us (39%)
  Pallas kernels  69.2 us (15%)
  other arithmetic  66.1 us (14%)
  local copies, waits for them, and re-layouts  55.4 us (12%)
  starting transfers between devices  48.9 us (11%)
  matrix products  34.8 us (8%)
    ppermute x19, waiting for transfers between devices, ctx_swap(): return lax.ppermute(value, 'ctx', CTX_PAIRS)  63.5 us
    ppermute x9, waiting for transfers between devices, ring_scatter(): arrived = lax.ppermute(total, 'shard', up)  51.6 us
    pallas_call x2, Pallas kernels, attention_back(): pl.pallas_call(bwd_kernel, grid=(keys // KTILE,), out_shape=[jax.ShapeDty...  35.2 us
    ppermute x9, waiting for transfers between devices, ring_gather(): pieces.append(lax.ppermute(pieces[-1], 'shard', down))  28.4 us
    ppermute x4, waiting for transfers between devices, tp_sum(): lax.ppermute(near, 'tp', FAR_PAIRS).astype(f32)  24.6 us
    ppermute x9, starting transfers between devices, ring_gather(): pieces.append(lax.ppermute(pieces[-1], 'shard', down))  22.7 us
    dot_general x4, matrix products, dot_nn(): return jnp.dot(left, right, preferred_element_type=f32)  19.1 us
    unnamed x163, local copies, waits for them, and re-layouts  18.9 us
  transfers between devices with their start and end apart: 53, of which 32 were waited for; matrix products, arithmetic and copies ran while one was open for 23% of the time, Pallas kernels for 11%

profile of v1, /device:TPU:0, one launch (start us, length us, event | category | flops | bytes accessed | tf_op | source)
XLA Modules:
  0.0 457.1 jit_solution(2338792886315461503)
XLA Ops:
  2.7 5.1 %collective-permute-start = (bf16[128,1024]{1,0:T(8,128)(2,1)S(1)}, bf16[128,1024]{1,0:T(8,128)(2,1)S(1)}, u32[]{:S(2)}, u32[]{:S(2)}) collective-permute-start(bf16[128,1024]{1,0:T(8,128)(2,1)S(1)} %pad_maximum_fusion.5.refs_0_), channel_id=1, source_target_pairs={{0,24},{8,0},{16,8},{24,16},{1,25},{9,1},{17,9},{25,17},{2,26},{10... | collective-permute-start | bytes 786440 | tf_op jit(solution)/shard_map/ppermute | solution.py:56
  7.8 5.6 %collective-permute-done.refs_1_ = bf16[128,1024]{1,0:T(8,128)(2,1)S(1)} collective-permute-done((bf16[128,1024]{1,0:T(8,128)(2,1)S(1)}, bf16[128,1024]{1,0:T(8,128)(2,1)S(1)}, u32[]{:S(2)}, u32[]{:S(2)}) %collective-permute-start) | collective-permute-done | bytes 262176 | tf_op jit(solution)/shard_map/ppermute | solution.py:56
  13.4 4.3 collective-permute-start.1
  19.1 3.2 collective-permute-done.1.refs_2_
  22.3 4.3 collective-permute-start.2
  32.7 4.9 %collective-permute-done.4.refs_5_ = bf16[128,1024]{1,0:T(8,128)(2,1)S(1)} collective-permute-done((bf16[128,1024]{1,0:T(8,128)(2,1)S(1)}, bf16[128,1024]{1,0:T(8,128)(2,1)S(1)}, u32[]{:S(2)}, u32[]{:S(2)}) %collective-permute-start.4) | collective-permute-done | bytes 262176 | tf_op jit(solution)/shard_map/ppermute | solution.py:49
  37.7 5.2 %collective-permute-done.5.refs_6_ = bf16[128,1024]{1,0:T(8,128)(2,1)S(1)} collective-permute-done((bf16[128,1024]{1,0:T(8,128)(2,1)S(1)}, bf16[128,1024]{1,0:T(8,128)(2,1)S(1)}, u32[]{:S(2)}, u32[]{:S(2)}) %collective-permute-start.5) | collective-permute-done | bytes 262176 | tf_op jit(solution)/shard_map/ppermute | solution.py:49
  42.8 2.8 collective-permute-done.6.refs_7_
  50.8 8.9 %collective-permute-done.7.refs_1_ = bf16[128,1024]{1,0:T(8,128)(2,1)S(1)} collective-permute-done((bf16[128,1024]{1,0:T(8,128)(2,1)S(1)}, bf16[128,1024]{1,0:T(8,128)(2,1)S(1)}, u32[]{:S(2)}, u32[]{:S(2)}) %collective-permute-start.7) | collective-permute-done | bytes 262176 | tf_op jit(solution)/shard_map/ppermute | solution.py:56
  59.7 2.1 collective-permute-start.8
  61.8 3.6 collective-permute-done.10.refs_1_
  65.5 2.1 collective-permute-start.11
  67.5 3.5 collective-permute-done.8.refs_2_
  71.1 2.1 collective-permute-start.9
  73.2 3.5 collective-permute-done.11.refs_2_
  76.7 2.4 collective-permute-start.12
  79.1 14.1 %attention_near.1 = (f32[784,256]{1,0:T(8,128)S(1)}, f32[784,256]{1,0:T(8,128)S(1)}, f32[784,256]{1,0:T(8,128)S(1)}) custom-call(bf16[784,256]{1,0:T(8,128)(2,1)S(1)} %get-tuple-element.82.q_ref, bf16[784,512]{1,0:T(8,128)(2,1)} %pad_maximum_fusion.2.kv_ref.k_ref.v_ref), custom_call_target="tpu_custom_call" | custom-call | flops 2517630976 | bytes 4194304 | tf_op jit(solution)/shard_map/attention_near/pallas_call | solution.py:173
  94.2 17.0 %attention_far.1 = (bf16[784,256]{1,0:T(8,128)(2,1)S(1)}, f32[784,128]{1,0:T(8,128)S(1)}) custom-call(bf16[784,256]{1,0:T(8,128)(2,1)S(1)} %copy-done.2, bf16[784,512]{1,0:T(8,128)(2,1)} %collective-permute-done.13.kv_ref.k_ref.v_ref, f32[784,256]{1,0:T(8,128)S(1)} %get-tuple-element.38.o_ref, f32[784,256]{1,0:T(8,128)S(1)} %get-tuple-element.39.m_ref, ...), custom_call_target="tpu_custom_call" | custom-call | flops 2517630976 | bytes 4194304 | tf_op jit(solution)/shard_map/attention_far/pallas_call | solution.py:188
  113.9 2.6 collective-permute-done.14
  119.8 18.4 %collective-permute-done.15 = bf16[392,1024]{1,0:T(8,128)(2,1)S(1)} collective-permute-done((bf16[392,1024]{1,0:T(8,128)(2,1)S(1)}, bf16[392,1024]{1,0:T(8,128)(2,1)S(1)}, u32[]{:S(2)}, u32[]{:S(2)}) %collective-permute-start.15) | collective-permute-done | bytes 802848 | tf_op jit(solution)/shard_map/ppermute | solution.py:105
  143.5 5.0 %collective-permute-done.17.refs_4_ = bf16[128,1024]{1,0:T(8,128)(2,1)S(1)} collective-permute-done((bf16[128,1024]{1,0:T(8,128)(2,1)S(1)}, bf16[128,1024]{1,0:T(8,128)(2,1)S(1)}, u32[]{:S(2)}, u32[]{:S(2)}) %collective-permute-start.17) | collective-permute-done | bytes 262176 | tf_op jit(solution)/shard_map/ppermute | solution.py:49
  149.8 4.4 collective-permute-done.18.refs_5_
  155.4 4.4 collective-permute-done.19.refs_6_
  161.0 4.4 collective-permute-done.20.refs_7_
  174.4 2.4 collective-permute-done.22.refs_5_
  176.8 5.6 %collective-permute-done.23.refs_6_ = bf16[128,1024]{1,0:T(8,128)(2,1)} collective-permute-done((bf16[128,1024]{1,0:T(8,128)(2,1)}, bf16[128,1024]{1,0:T(8,128)(2,1)}, u32[]{:S(2)}, u32[]{:S(2)}) %collective-permute-start.23) | collective-permute-done | bytes 262176 | tf_op jit(solution)/shard_map/ppermute | solution.py:49
  182.4 5.2 %collective-permute-done.24.refs_7_ = bf16[128,1024]{1,0:T(8,128)(2,1)} collective-permute-done((bf16[128,1024]{1,0:T(8,128)(2,1)}, bf16[128,1024]{1,0:T(8,128)(2,1)}, u32[]{:S(2)}, u32[]{:S(2)}) %collective-permute-start.24) | collective-permute-done | bytes 262176 | tf_op jit(solution)/shard_map/ppermute | solution.py:49
  189.2 3.5 fusion.41
  192.7 3.0 multiply_reduce_fusion
  195.8 12.4 %multiply_convert_fusion = (bf16[784,1024]{1,0:T(8,128)(2,1)S(1)}, f32[784,1024]{1,0:T(8,128)S(1)}, f32[784,1024]{1,0:T(8,128)S(1)}) fusion(f32[1024]{0:T(1024)S(1)} %convert_element_type.355, bf16[1024,1024]{1,0:T(8,128)(2,1)S(1)} %assemble.4, f32[1024]{0:T(1024)S(1)} %convert_element_type.353, f32[1024]{0:T(1024)S(1)} %convert_element_type.352, ...), kind=kOutput, calls=%fused_computation.58 | convolution fusion | flops 1711603712 | bytes 13359233 | tf_op jit(solution)/shard_map/dot_general | solution.py:37
  208.2 3.5 convert_reduce_fusion.5
  211.7 1.9 convolution_convert_fusion.2
  215.0 2.4 fusion.44
  217.4 2.0 copy-done.37
  222.2 4.1 convolution_convert_fusion.3
  229.9 2.9 copy.45
  236.2 10.2 %collective-permute-done.49 = bf16[4,128,1024]{1,2,0:T(8,128)(2,1)} collective-permute-done((bf16[4,128,1024]{1,2,0:T(8,128)(2,1)}, bf16[4,128,1024]{1,2,0:T(8,128)(2,1)}, u32[]{:S(2)}, u32[]{:S(2)}) %collective-permute-start.49) | collective-permute-done | bytes 1048608 | tf_op jit(solution)/shard_map/ppermute | solution.py:49
  249.9 7.4 %collective-permute-done.50 = bf16[128,1024]{0,1:T(8,128)(2,1)S(1)} collective-permute-done((bf16[128,1024]{0,1:T(8,128)(2,1)S(1)}, bf16[128,1024]{0,1:T(8,128)(2,1)S(1)}, u32[]{:S(2)}, u32[]{:S(2)}) %collective-permute-start.50) | collective-permute-done | bytes 262176 | tf_op jit(solution)/shard_map/ppermute | solution.py:71
  257.9 8.0 %collective-permute-done.51 = bf16[128,1024]{0,1:T(8,128)(2,1)S(1)} collective-permute-done((bf16[128,1024]{0,1:T(8,128)(2,1)S(1)}, bf16[128,1024]{0,1:T(8,128)(2,1)S(1)}, u32[]{:S(2)}, u32[]{:S(2)}) %collective-permute-start.51) | collective-permute-done | bytes 262176 | tf_op jit(solution)/shard_map/ppermute | solution.py:71
  266.1 6.2 %collective-permute-done.26 = bf16[392,1024]{1,0:T(8,128)(2,1)S(1)} collective-permute-done((bf16[392,1024]{1,0:T(8,128)(2,1)S(1)}, bf16[392,1024]{1,0:T(8,128)(2,1)S(1)}, u32[]{:S(2)}, u32[]{:S(2)}) %collective-permute-start.26) | collective-permute-done | bytes 802848 | tf_op jit(solution)/shard_map/ppermute | solution.py:105
  275.1 3.6 fusion.12
  278.7 3.7 fusion.73
  282.5 6.9 %convert_reduce_fusion.2 = (f32[1024]{0:T(1024)S(1)}, f32[1024]{0:T(1024)S(1)}, bf16[1024,784]{0,1:T(8,128)(2,1)}) fusion(bf16[392,1024]{1,0:T(8,128)(2,1)S(1)} %add_convert_fusion.5, bf16[392,1024]{1,0:T(8,128)(2,1)S(1)} %collective-permute-done.30, pred[]{:T(512)S(6)} %eq.23, f32[784]{0:T(1024)S(1)} %copy-done.52, f32[784]{0:T(1024)S(1)} %broadcast_multiply_fusion, ...), kind=kLoop, calls=%fused_computation.11 | loop fusion | flops 24885248 | bytes 6449281 | tf_op jit(solution)/shard_map/transpose(jvp())/reduce_sum | solution.py:33
  289.4 5.3 %dot_general.56 = bf16[4,2,128,784]{2,1,0,3:T(2,128)(2,1)} reshape(bf16[1024,784]{0,1:T(8,128)(2,1)} %get-tuple-element.81) | data formatting | bytes 3211264 | tf_op jit(solution)/shard_map/dot_general | solution.py:41
  294.7 6.3 %convert_reduce_fusion.4 = (f32[1024]{0:T(1024)S(1)}, bf16[784,1024]{1,0:T(8,128)(2,1)S(1)}, f32[1024]{0:T(1024)S(1)}) fusion(f32[784]{0:T(1024)S(1)} %negate_multiply_fusion.2, f32[784]{0:T(1024)S(1)} %multiply_multiply_fusion.6, f32[784]{0:T(1024)S(1)} %broadcast_multiply_fusion, f32[1024]{0:T(1024)S(1)} %convert_element_type.350, ...), kind=kLoop, calls=%fused_computation.55 | loop fusion | flops 28899328 | bytes 8057089 | tf_op jit(solution)/shard_map/reduce_sum | solution.py:334
  303.7 2.4 copy.41
  307.4 17.5 %attention_back.2 = (f32[784,512]{1,0:T(8,128)S(1)}, f32[784,256]{1,0:T(8,128)S(1)}) custom-call(bf16[784,512]{1,0:T(8,128)(2,1)} %collective-permute-done.13.kv_ref.k_ref.v_ref, bf16[784,512]{1,0:T(8,128)(2,1)} %collective-permute-done.13.kv_ref.k_ref.v_ref, bf16[784,256]{1,0:T(8,128)(2,1)S(1)} %copy-done.3, bf16[784,256]{1,0:T(8,128)(2,1)S(1)} %get-tuple-element.99.do_ref, ...), custom_call_target="tpu_custom_call" | custom-call | flops 6294077440 | bytes 4194304 | tf_op jit(solution)/shard_map/attention_back/pallas_call | solution.py:230
  326.1 17.7 %attention_back.3 = (f32[784,512]{1,0:T(8,128)S(1)}, f32[784,256]{1,0:T(8,128)S(1)}) custom-call(bf16[784,512]{1,0:T(8,128)(2,1)} %pad_maximum_fusion.2.kv_ref.k_ref.v_ref, bf16[784,512]{1,0:T(8,128)(2,1)} %pad_maximum_fusion.2.kv_ref.k_ref.v_ref, bf16[784,256]{1,0:T(8,128)(2,1)S(1)} %copy-done.3, bf16[784,256]{1,0:T(8,128)(2,1)S(1)} %get-tuple-element.99.do_ref, ...), custom_call_target="tpu_custom_call" | custom-call | flops 6294077440 | bytes 4194304 | tf_op jit(solution)/shard_map/attention_back/pallas_call | solution.py:230
  343.8 4.5 add_convert_fusion
  348.3 2.4 fusion.42
  355.6 4.6 %collective-permute-done.44 = f32[5120]{0:T(1024)S(1)} collective-permute-done((f32[5120]{0:T(1024)S(1)}, f32[5120]{0:T(1024)S(1)}, u32[]{:S(2)}, u32[]{:S(2)}) %collective-permute-start.44) | collective-permute-done | bytes 20512 | tf_op jit(solution)/shard_map/ppermute | solution.py:115
  363.5 2.1 fusion.55
  365.6 2.7 pad_maximum_fusion
  368.3 6.9 %reshape.494 = f32[4,2,128,1024]{2,1,0,3:T(2,128)} reshape(f32[1024,1024]{0,1:T(8,128)} %pad_maximum_fusion) | data formatting | bytes 8388608 | tf_op jit(solution)/shard_map/reshape | solution.py:317
  375.2 4.2 constant_dynamic-slice_fusion.2
  384.8 8.3 %collective-permute-done.46 = bf16[128,1024]{1,0:T(8,128)(2,1)S(1)} collective-permute-done((bf16[128,1024]{1,0:T(8,128)(2,1)S(1)}, bf16[128,1024]{1,0:T(8,128)(2,1)S(1)}, u32[]{:S(2)}, u32[]{:S(2)}) %collective-permute-start.46) | collective-permute-done | bytes 262176 | tf_op jit(solution)/shard_map/ppermute | solution.py:71
  396.3 8.9 %collective-permute-done.35 = bf16[4,128,1024]{1,2,0:T(8,128)(2,1)S(1)} collective-permute-done((bf16[4,128,1024]{1,2,0:T(8,128)(2,1)S(1)}, bf16[4,128,1024]{1,2,0:T(8,128)(2,1)S(1)}, u32[]{:S(2)}, u32[]{:S(2)}) %collective-permute-start.35) | collective-permute-done | bytes 1048608 | tf_op jit(solution)/shard_map/ppermute | solution.py:49
  406.7 9.9 %collective-permute-done.36 = bf16[128,1024]{0,1:T(8,128)(2,1)S(1)} collective-permute-done((bf16[128,1024]{0,1:T(8,128)(2,1)S(1)}, bf16[128,1024]{0,1:T(8,128)(2,1)S(1)}, u32[]{:S(2)}, u32[]{:S(2)}) %collective-permute-start.36) | collective-permute-done | bytes 262176 | tf_op jit(solution)/shard_map/ppermute | solution.py:71
  417.1 9.4 %collective-permute-done.37 = bf16[128,1024]{0,1:T(8,128)(2,1)S(1)} collective-permute-done((bf16[128,1024]{0,1:T(8,128)(2,1)S(1)}, bf16[128,1024]{0,1:T(8,128)(2,1)S(1)}, u32[]{:S(2)}, u32[]{:S(2)}) %collective-permute-start.37) | collective-permute-done | bytes 262176 | tf_op jit(solution)/shard_map/ppermute | solution.py:71
  427.6 7.8 %collective-permute-done.38 = bf16[128,1024]{0,1:T(8,128)(2,1)S(1)} collective-permute-done((bf16[128,1024]{0,1:T(8,128)(2,1)S(1)}, bf16[128,1024]{0,1:T(8,128)(2,1)S(1)}, u32[]{:S(2)}, u32[]{:S(2)}) %collective-permute-start.38) | collective-permute-done | bytes 262176 | tf_op jit(solution)/shard_map/ppermute | solution.py:71
  436.5 2.0 fusion.23
  441.0 1.9 copy.47
  443.0 3.7 collective-permute-done.40
  446.7 8.9 %fusion.22 = bf16[1,784,1024]{2,1,0:T(8,128)(2,1)} fusion(bf16[1,784,1024]{2,1,0:T(8,128)(2,1)S(1)} %copy-done.21, bf16[1,784,1024]{2,1,0:T(8,128)(2,1)} %param.29, bf16[1,392,1024]{2,1,0:T(8,128)(2,1)S(1)} %bitcast.196, bf16[1,392,1024]{2,1,0:T(8,128)(2,1)S(1)} %bitcast.195, bf16[1,392,1024]{2,1,0:T(8,128)(2,1)} %bitcast.198, ...), kind=kLoop, calls=%fused_computation.40 | loop fusion | flops 40943616 | bytes 9671169 | tf_op jit(solution)/shard_map/convert_element_type | solution.py:355
  (315 shorter events, 88.5 us)
Async XLA Ops:
  0.7 32.0 %copy-start.75 = (bf16[256]{0:T(256)(128)(2,1)S(1)}, bf16[256]{0:T(256)(128)(2,1)}, u32[]{:S(2)}) copy-start(bf16[256]{0:T(256)(128)(2,1)} %param.18) | copy-start | bytes 1540
  0.7 32.0 %copy-start.67 = (bf16[1024]{0:T(1024)(128)(2,1)S(1)}, bf16[1024]{0:T(1024)(128)(2,1)}, u32[]{:S(2)}) copy-start(bf16[1024]{0:T(1024)(128)(2,1)} %param.21) | copy-start | bytes 6148
  0.7 32.0 %copy-start.68 = (bf16[1024]{0:T(1024)(128)(2,1)S(1)}, bf16[1024]{0:T(1024)(128)(2,1)}, u32[]{:S(2)}) copy-start(bf16[1024]{0:T(1024)(128)(2,1)} %param.22) | copy-start | bytes 6148
  2.7 10.7 %collective-permute-start = (bf16[128,1024]{1,0:T(8,128)(2,1)S(1)}, bf16[128,1024]{1,0:T(8,128)(2,1)S(1)}, u32[]{:S(2)}, u32[]{:S(2)}) collective-permute-start(bf16[128,1024]{1,0:T(8,128)(2,1)S(1)} %pad_maximum_fusion.5.refs_0_), channel_id=1, source_target_pairs={{0,24},{8,0},{16,8},{24,16},{1,25},{9,1},{17,9},{25,17},{2,26},{10... | collective-permute-start | bytes 786440 | tf_op jit(solution)/shard_map/ppermute | solution.py:56
  13.4 9.0 %collective-permute-start.1 = (bf16[128,1024]{1,0:T(8,128)(2,1)S(1)}, bf16[128,1024]{1,0:T(8,128)(2,1)S(1)}, u32[]{:S(2)}, u32[]{:S(2)}) collective-permute-start(bf16[128,1024]{1,0:T(8,128)(2,1)S(1)} %collective-permute-done.refs_1_), channel_id=1, source_target_pairs={{0,24},{8,0},{16,8},{24,16},{1,25},{9,1},{17,9},{25,17},{2,26},{10... | collective-permute-start | bytes 786440 | tf_op jit(solution)/shard_map/ppermute | solution.py:56
  17.7 15.1 %collective-permute-start.3 = (bf16[128,1024]{1,0:T(8,128)(2,1)S(1)}, bf16[128,1024]{1,0:T(8,128)(2,1)S(1)}, u32[]{:S(2)}, u32[]{:S(2)}) collective-permute-start(bf16[128,1024]{1,0:T(8,128)(2,1)S(1)} %pad_maximum_fusion.5.refs_0_), channel_id=1, source_target_pairs={{0,4},{4,0},{1,5},{5,1},{2,6},{6,2},{3,7},{7,3},{8,12},{12,8},{9,1... | collective-permute-start | bytes 786440 | tf_op jit(solution)/shard_map/ppermute | solution.py:49
  22.3 8.2 %collective-permute-start.2 = (bf16[128,1024]{1,0:T(8,128)(2,1)S(1)}, bf16[128,1024]{1,0:T(8,128)(2,1)S(1)}, u32[]{:S(2)}, u32[]{:S(2)}) collective-permute-start(bf16[128,1024]{1,0:T(8,128)(2,1)S(1)} %collective-permute-done.1.refs_2_), channel_id=1, source_target_pairs={{0,24},{8,0},{16,8},{24,16},{1,25},{9,1},{17,9},{25,17},{2,26},{10... | collective-permute-start | bytes 786440 | tf_op jit(solution)/shard_map/ppermute | solution.py:56
  28.4 9.3 %collective-permute-start.4 = (bf16[128,1024]{1,0:T(8,128)(2,1)S(1)}, bf16[128,1024]{1,0:T(8,128)(2,1)S(1)}, u32[]{:S(2)}, u32[]{:S(2)}) collective-permute-start(bf16[128,1024]{1,0:T(8,128)(2,1)S(1)} %collective-permute-done.refs_1_), channel_id=1, source_target_pairs={{0,4},{4,0},{1,5},{5,1},{2,6},{6,2},{3,7},{7,3},{8,12},{12,8},{9,1... | collective-permute-start | bytes 786440 | tf_op jit(solution)/shard_map/ppermute | solution.py:49
  29.9 12.9 %collective-permute-start.5 = (bf16[128,1024]{1,0:T(8,128)(2,1)S(1)}, bf16[128,1024]{1,0:T(8,128)(2,1)S(1)}, u32[]{:S(2)}, u32[]{:S(2)}) collective-permute-start(bf16[128,1024]{1,0:T(8,128)(2,1)S(1)} %collective-permute-done.1.refs_2_), channel_id=1, source_target_pairs={{0,4},{4,0},{1,5},{5,1},{2,6},{6,2},{3,7},{7,3},{8,12},{12,8},{9,1... | collective-permute-start | bytes 786440 | tf_op jit(solution)/shard_map/ppermute | solution.py:49
  30.5 15.1 %collective-permute-start.6 = (bf16[128,1024]{1,0:T(8,128)(2,1)S(1)}, bf16[128,1024]{1,0:T(8,128)(2,1)S(1)}, u32[]{:S(2)}, u32[]{:S(2)}) collective-permute-start(bf16[128,1024]{1,0:T(8,128)(2,1)S(1)} %collective-permute-done.2.refs_3_), channel_id=1, source_target_pairs={{0,4},{4,0},{1,5},{5,1},{2,6},{6,2},{3,7},{7,3},{8,12},{12,8},{9,1... | collective-permute-start | bytes 786440 | tf_op jit(solution)/shard_map/ppermute | solution.py:49
  47.8 45.4 %copy-start.1 = (bf16[784,256]{1,0:T(8,128)(2,1)}, bf16[784,256]{1,0:T(8,128)(2,1)S(1)}, u32[]{:S(2)}) copy-start(bf16[784,256]{1,0:T(8,128)(2,1)S(1)} %get-tuple-element.82.q_ref) | copy-start | bytes 1204228
  48.8 44.4 %collective-permute-start.13 = (bf16[784,512]{1,0:T(8,128)(2,1)}, bf16[784,512]{1,0:T(8,128)(2,1)}, u32[]{:S(2)}, u32[]{:S(2)}) collective-permute-start(bf16[784,512]{1,0:T(8,128)(2,1)} %pad_maximum_fusion.2.kv_ref.k_ref.v_ref), channel_id=1, source_target_pairs={{0,4},{4,0},{1,5},{5,1},{2,6},{6,2},{3,7},{7,3},{8,12},{12,8},{9,1... | collective-permute-start | bytes 2408456 | tf_op jit(solution)/shard_map/ppermute | solution.py:49
  50.4 9.3 %collective-permute-start.7 = (bf16[128,1024]{1,0:T(8,128)(2,1)S(1)}, bf16[128,1024]{1,0:T(8,128)(2,1)S(1)}, u32[]{:S(2)}, u32[]{:S(2)}) collective-permute-start(bf16[128,1024]{1,0:T(8,128)(2,1)S(1)} %copy-done.4), channel_id=1, source_target_pairs={{0,24},{8,0},{16,8},{24,16},{1,25},{9,1},{17,9},{25,17},{2,26},{10... | collective-permute-start | bytes 786440 | tf_op jit(solution)/shard_map/ppermute | solution.py:56
  50.8 14.7 %collective-permute-start.10 = (bf16[128,1024]{1,0:T(8,128)(2,1)S(1)}, bf16[128,1024]{1,0:T(8,128)(2,1)}, u32[]{:S(2)}, u32[]{:S(2)}) collective-permute-start(bf16[128,1024]{1,0:T(8,128)(2,1)S(1)} %bitcast.190), channel_id=1, source_target_pairs={{0,24},{8,0},{16,8},{24,16},{1,25},{9,1},{17,9},{25,17},{2,26},{10... | collective-permute-start | bytes 786440 | tf_op jit(solution)/shard_map/ppermute | solution.py:56
  59.7 33.4 %copy-start.5 = (bf16[128,1024]{1,0:T(8,128)(2,1)}, bf16[128,1024]{1,0:T(8,128)(2,1)S(1)}, u32[]{:S(2)}) copy-start(bf16[128,1024]{1,0:T(8,128)(2,1)S(1)} %collective-permute-done.7.refs_1_) | copy-start | bytes 786436
  59.7 11.3 %collective-permute-start.8 = (bf16[128,1024]{1,0:T(8,128)(2,1)S(1)}, bf16[128,1024]{1,0:T(8,128)(2,1)}, u32[]{:S(2)}, u32[]{:S(2)}) collective-permute-start(bf16[128,1024]{1,0:T(8,128)(2,1)S(1)} %collective-permute-done.7.refs_1_), channel_id=1, source_target_pairs={{0,24},{8,0},{16,8},{24,16},{1,25},{9,1},{17,9},{25,17},{2,26},{10... | collective-permute-start | bytes 786440 | tf_op jit(solution)/shard_map/ppermute | solution.py:56
  65.5 11.2 %collective-permute-start.11 = (bf16[128,1024]{1,0:T(8,128)(2,1)}, bf16[128,1024]{1,0:T(8,128)(2,1)}, u32[]{:S(2)}, u32[]{:S(2)}) collective-permute-start(bf16[128,1024]{1,0:T(8,128)(2,1)} %collective-permute-done.10.refs_1_), channel_id=1, source_target_pairs={{0,24},{8,0},{16,8},{24,16},{1,25},{9,1},{17,9},{25,17},{2,26},{10... | collective-permute-start | bytes 786440 | tf_op jit(solution)/shard_map/ppermute | solution.py:56
  71.1 22.1 %collective-permute-start.9 = (bf16[128,1024]{1,0:T(8,128)(2,1)}, bf16[128,1024]{1,0:T(8,128)(2,1)}, u32[]{:S(2)}, u32[]{:S(2)}) collective-permute-start(bf16[128,1024]{1,0:T(8,128)(2,1)} %collective-permute-done.8.refs_2_), channel_id=1, source_target_pairs={{0,24},{8,0},{16,8},{24,16},{1,25},{9,1},{17,9},{25,17},{2,26},{10... | collective-permute-start | bytes 786440 | tf_op jit(solution)/shard_map/ppermute | solution.py:56
  76.7 16.5 %collective-permute-start.12 = (bf16[128,1024]{1,0:T(8,128)(2,1)}, bf16[128,1024]{1,0:T(8,128)(2,1)}, u32[]{:S(2)}, u32[]{:S(2)}) collective-permute-start(bf16[128,1024]{1,0:T(8,128)(2,1)} %collective-permute-done.11.refs_2_), channel_id=1, source_target_pairs={{0,24},{8,0},{16,8},{24,16},{1,25},{9,1},{17,9},{25,17},{2,26},{10... | collective-permute-start | bytes 786440 | tf_op jit(solution)/shard_map/ppermute | solution.py:56
  113.0 53.7 %copy-start.69 = (bf16[1024]{0:T(1024)(128)(2,1)S(1)}, bf16[1024]{0:T(1024)(128)(2,1)}, u32[]{:S(2)}) copy-start(bf16[1024]{0:T(1024)(128)(2,1)} %param.20) | copy-start | bytes 6148
  113.0 53.7 %copy-start.70 = (bf16[1024]{0:T(1024)(128)(2,1)S(1)}, bf16[1024]{0:T(1024)(128)(2,1)}, u32[]{:S(2)}) copy-start(bf16[1024]{0:T(1024)(128)(2,1)} %param.23) | copy-start | bytes 6148
  113.0 53.7 %copy-start.71 = (bf16[1024]{0:T(1024)(128)(2,1)S(1)}, bf16[1024]{0:T(1024)(128)(2,1)}, u32[]{:S(2)}) copy-start(bf16[1024]{0:T(1024)(128)(2,1)} %param.24) | copy-start | bytes 6148
  113.0 53.8 %copy-start.72 = (bf16[1024]{0:T(1024)(128)(2,1)S(1)}, bf16[1024]{0:T(1024)(128)(2,1)}, u32[]{:S(2)}) copy-start(bf16[1024]{0:T(1024)(128)(2,1)} %param.26) | copy-start | bytes 6148
  113.0 53.8 %copy-start.73 = (bf16[1024]{0:T(1024)(128)(2,1)S(1)}, bf16[1024]{0:T(1024)(128)(2,1)}, u32[]{:S(2)}) copy-start(bf16[1024]{0:T(1024)(128)(2,1)} %param.28) | copy-start | bytes 6148
  113.9 2.7 collective-permute-start.14
  118.3 20.0 %collective-permute-start.15 = (bf16[392,1024]{1,0:T(8,128)(2,1)S(1)}, bf16[392,1024]{1,0:T(8,128)(2,1)S(1)}, u32[]{:S(2)}, u32[]{:S(2)}) collective-permute-start(bf16[392,1024]{1,0:T(8,128)(2,1)S(1)} %add_convert_fusion.10), channel_id=1, source_target_pairs={{0,2},{2,0},{1,3},{3,1},{4,6},{6,4},{5,7},{7,5},{8,10},{10,8},{9,1... | collective-permute-start | bytes 2408456 | tf_op jit(solution)/shard_map/ppermute | solution.py:105
  139.5 49.7 %collective-permute-start.16 = (bf16[392,1024]{1,0:T(8,128)(2,1)}, bf16[392,1024]{1,0:T(8,128)(2,1)}, u32[]{:S(2)}, u32[]{:S(2)}) collective-permute-start(bf16[392,1024]{1,0:T(8,128)(2,1)} %add_convert_fusion.9), channel_id=1, source_target_pairs={{0,1},{1,0},{2,3},{3,2},{4,5},{5,4},{6,7},{7,6},{8,9},{9,8},{10,11... | collective-permute-start | bytes 2408456 | tf_op jit(solution)/shard_map/ppermute | solution.py:107
  139.5 9.1 %collective-permute-start.17 = (bf16[128,1024]{1,0:T(8,128)(2,1)S(1)}, bf16[128,1024]{1,0:T(8,128)(2,1)S(1)}, u32[]{:S(2)}, u32[]{:S(2)}) collective-permute-start(bf16[128,1024]{1,0:T(8,128)(2,1)S(1)} %copy-done.4), channel_id=1, source_target_pairs={{0,4},{4,0},{1,5},{5,1},{2,6},{6,2},{3,7},{7,3},{8,12},{12,8},{9,1... | collective-permute-start | bytes 786440 | tf_op jit(solution)/shard_map/ppermute | solution.py:49
  140.0 14.2 %collective-permute-start.18 = (bf16[128,1024]{1,0:T(8,128)(2,1)S(1)}, bf16[128,1024]{1,0:T(8,128)(2,1)S(1)}, u32[]{:S(2)}, u32[]{:S(2)}) collective-permute-start(bf16[128,1024]{1,0:T(8,128)(2,1)S(1)} %copy-done.6), channel_id=1, source_target_pairs={{0,4},{4,0},{1,5},{5,1},{2,6},{6,2},{3,7},{7,3},{8,12},{12,8},{9,1... | collective-permute-start | bytes 786440 | tf_op jit(solution)/shard_map/ppermute | solution.py:49
  141.5 18.3 %collective-permute-start.19 = (bf16[128,1024]{1,0:T(8,128)(2,1)}, bf16[128,1024]{1,0:T(8,128)(2,1)S(1)}, u32[]{:S(2)}, u32[]{:S(2)}) collective-permute-start(bf16[128,1024]{1,0:T(8,128)(2,1)} %collective-permute-done.8.refs_2_), channel_id=1, source_target_pairs={{0,4},{4,0},{1,5},{5,1},{2,6},{6,2},{3,7},{7,3},{8,12},{12,8},{9,1... | collective-permute-start | bytes 786440 | tf_op jit(solution)/shard_map/ppermute | solution.py:49
  142.0 23.4 %collective-permute-start.20 = (bf16[128,1024]{1,0:T(8,128)(2,1)}, bf16[128,1024]{1,0:T(8,128)(2,1)S(1)}, u32[]{:S(2)}, u32[]{:S(2)}) collective-permute-start(bf16[128,1024]{1,0:T(8,128)(2,1)} %collective-permute-done.9.refs_3_), channel_id=1, source_target_pairs={{0,4},{4,0},{1,5},{5,1},{2,6},{6,2},{3,7},{7,3},{8,12},{12,8},{9,1... | collective-permute-start | bytes 786440 | tf_op jit(solution)/shard_map/ppermute | solution.py:49
  149.3 25.1 %collective-permute-start.21 = (bf16[128,1024]{1,0:T(8,128)(2,1)S(1)}, bf16[128,1024]{1,0:T(8,128)(2,1)}, u32[]{:S(2)}, u32[]{:S(2)}) collective-permute-start(bf16[128,1024]{1,0:T(8,128)(2,1)S(1)} %bitcast.191), channel_id=1, source_target_pairs={{0,4},{4,0},{1,5},{5,1},{2,6},{6,2},{3,7},{7,3},{8,12},{12,8},{9,1... | collective-permute-start | bytes 786440 | tf_op jit(solution)/shard_map/ppermute | solution.py:49
  154.9 21.9 %collective-permute-start.22 = (bf16[128,1024]{1,0:T(8,128)(2,1)}, bf16[128,1024]{1,0:T(8,128)(2,1)}, u32[]{:S(2)}, u32[]{:S(2)}) collective-permute-start(bf16[128,1024]{1,0:T(8,128)(2,1)} %collective-permute-done.10.refs_1_), channel_id=1, source_target_pairs={{0,4},{4,0},{1,5},{5,1},{2,6},{6,2},{3,7},{7,3},{8,12},{12,8},{9,1... | collective-permute-start | bytes 786440 | tf_op jit(solution)/shard_map/ppermute | solution.py:49
  160.5 21.9 %collective-permute-start.23 = (bf16[128,1024]{1,0:T(8,128)(2,1)}, bf16[128,1024]{1,0:T(8,128)(2,1)}, u32[]{:S(2)}, u32[]{:S(2)}) collective-permute-start(bf16[128,1024]{1,0:T(8,128)(2,1)} %collective-permute-done.11.refs_2_), channel_id=1, source_target_pairs={{0,4},{4,0},{1,5},{5,1},{2,6},{6,2},{3,7},{7,3},{8,12},{12,8},{9,1... | collective-permute-start | bytes 786440 | tf_op jit(solution)/shard_map/ppermute | solution.py:49
  166.1 21.5 %collective-permute-start.24 = (bf16[128,1024]{1,0:T(8,128)(2,1)}, bf16[128,1024]{1,0:T(8,128)(2,1)}, u32[]{:S(2)}, u32[]{:S(2)}) collective-permute-start(bf16[128,1024]{1,0:T(8,128)(2,1)} %collective-permute-done.12.refs_3_), channel_id=1, source_target_pairs={{0,4},{4,0},{1,5},{5,1},{2,6},{6,2},{3,7},{7,3},{8,12},{12,8},{9,1... | collective-permute-start | bytes 786440 | tf_op jit(solution)/shard_map/ppermute | solution.py:49
  214.7 18.2 %collective-permute-start.28 = (bf16[392,1024]{1,0:T(8,128)(2,1)}, bf16[392,1024]{1,0:T(8,128)(2,1)}, u32[]{:S(2)}, u32[]{:S(2)}) collective-permute-start(bf16[392,1024]{1,0:T(8,128)(2,1)} %constant_dynamic-slice_fusion.5), channel_id=1, source_target_pairs={{0,1},{1,0},{2,3},{3,2},{4,5},{5,4},{6,7},{7,6},{8,9},{9,8},{10,11... | collective-permute-start | bytes 2408456 | tf_op jit(solution)/shard_map/ppermute | solution.py:103
  220.9 25.6 %collective-permute-start.49 = (bf16[4,128,1024]{1,2,0:T(8,128)(2,1)}, bf16[4,128,1024]{1,2,0:T(8,128)(2,1)}, u32[]{:S(2)}, u32[]{:S(2)}) collective-permute-start(bf16[4,128,1024]{1,2,0:T(8,128)(2,1)} %bitcast.203), channel_id=1, source_target_pairs={{0,4},{4,0},{1,5},{5,1},{2,6},{6,2},{3,7},{7,3},{8,12},{12,8},{9,1... | collective-permute-start | bytes 3145736 | tf_op jit(solution)/shard_map/ppermute | solution.py:49
  228.4 19.6 %collective-permute-start.25 = (bf16[392,1024]{1,0:T(8,128)(2,1)}, bf16[392,1024]{1,0:T(8,128)(2,1)S(1)}, u32[]{:S(2)}, u32[]{:S(2)}) collective-permute-start(bf16[392,1024]{1,0:T(8,128)(2,1)} %constant_dynamic-slice_fusion.6), channel_id=1, source_target_pairs={{0,1},{1,0},{2,3},{3,2},{4,5},{5,4},{6,7},{7,6},{8,9},{9,8},{10,11... | collective-permute-start | bytes 2408456 | tf_op jit(solution)/shard_map/ppermute | solution.py:103
  234.7 22.9 %collective-permute-start.29 = (bf16[392,1024]{1,0:T(8,128)(2,1)S(1)}, bf16[392,1024]{1,0:T(8,128)(2,1)S(1)}, u32[]{:S(2)}, u32[]{:S(2)}) collective-permute-start(bf16[392,1024]{1,0:T(8,128)(2,1)S(1)} %add_convert_fusion.6), channel_id=1, source_target_pairs={{0,2},{2,0},{1,3},{3,1},{4,6},{6,4},{5,7},{7,5},{8,10},{10,8},{9,1... | collective-permute-start | bytes 2408456 | tf_op jit(solution)/shard_map/ppermute | solution.py:105
  247.9 9.4 %collective-permute-start.50 = (bf16[128,1024]{0,1:T(8,128)(2,1)S(1)}, bf16[128,1024]{0,1:T(8,128)(2,1)S(1)}, u32[]{:S(2)}, u32[]{:S(2)}) collective-permute-start(bf16[128,1024]{0,1:T(8,128)(2,1)S(1)} %fusion.67), channel_id=1, source_target_pairs={{0,8},{8,16},{16,24},{24,0},{1,9},{9,17},{17,25},{25,1},{2,10},{10... | collective-permute-start | bytes 786440 | tf_op jit(solution)/shard_map/ppermute | solution.py:71
  248.3 23.9 %collective-permute-start.26 = (bf16[392,1024]{1,0:T(8,128)(2,1)S(1)}, bf16[392,1024]{1,0:T(8,128)(2,1)S(1)}, u32[]{:S(2)}, u32[]{:S(2)}) collective-permute-start(bf16[392,1024]{1,0:T(8,128)(2,1)S(1)} %add_convert_fusion.8), channel_id=1, source_target_pairs={{0,2},{2,0},{1,3},{3,1},{4,6},{6,4},{5,7},{7,5},{8,10},{10,8},{9,1... | collective-permute-start | bytes 2408456 | tf_op jit(solution)/shard_map/ppermute | solution.py:105
  257.4 8.5 %collective-permute-start.51 = (bf16[128,1024]{0,1:T(8,128)(2,1)S(1)}, bf16[128,1024]{0,1:T(8,128)(2,1)S(1)}, u32[]{:S(2)}, u32[]{:S(2)}) collective-permute-start(bf16[128,1024]{0,1:T(8,128)(2,1)S(1)} %fusion.56), channel_id=1, source_target_pairs={{0,8},{8,16},{16,24},{24,0},{1,9},{9,17},{17,25},{25,1},{2,10},{10... | collective-permute-start | bytes 786440 | tf_op jit(solution)/shard_map/ppermute | solution.py:71
  257.8 36.9 %copy-start.22 = (bf16[392,1024]{1,0:T(8,128)(2,1)}, bf16[392,1024]{1,0:T(8,128)(2,1)S(1)}, u32[]{:S(2)}) copy-start(bf16[392,1024]{1,0:T(8,128)(2,1)S(1)} %add_convert_fusion.5) | copy-start | bytes 2408452
  257.8 17.2 %collective-permute-start.30 = (bf16[392,1024]{1,0:T(8,128)(2,1)S(1)}, bf16[392,1024]{1,0:T(8,128)(2,1)S(1)}, u32[]{:S(2)}, u32[]{:S(2)}) collective-permute-start(bf16[392,1024]{1,0:T(8,128)(2,1)S(1)} %add_convert_fusion.5), channel_id=1, source_target_pairs={{0,1},{1,0},{2,3},{3,2},{4,5},{5,4},{6,7},{7,6},{8,9},{9,8},{10,11... | collective-permute-start | bytes 2408456 | tf_op jit(solution)/shard_map/ppermute | solution.py:107
  266.0 8.2 %collective-permute-start.52 = (bf16[128,1024]{0,1:T(8,128)(2,1)S(1)}, bf16[128,1024]{0,1:T(8,128)(2,1)S(1)}, u32[]{:S(2)}, u32[]{:S(2)}) collective-permute-start(bf16[128,1024]{0,1:T(8,128)(2,1)S(1)} %fusion.57), channel_id=1, source_target_pairs={{0,8},{8,16},{16,24},{24,0},{1,9},{9,17},{17,25},{25,1},{2,10},{10... | collective-permute-start | bytes 786440 | tf_op jit(solution)/shard_map/ppermute | solution.py:71
  273.4 70.3 %collective-permute-start.27 = (bf16[392,1024]{1,0:T(8,128)(2,1)}, bf16[392,1024]{1,0:T(8,128)(2,1)}, u32[]{:S(2)}, u32[]{:S(2)}) collective-permute-start(bf16[392,1024]{1,0:T(8,128)(2,1)} %add_convert_fusion.7), channel_id=1, source_target_pairs={{0,1},{1,0},{2,3},{3,2},{4,5},{5,4},{6,7},{7,6},{8,9},{9,8},{10,11... | collective-permute-start | bytes 2408456 | tf_op jit(solution)/shard_map/ppermute | solution.py:107
  301.1 50.4 %collective-permute-start.42 = (f32[5120]{0:T(1024)S(1)}, f32[5120]{0:T(1024)S(1)}, u32[]{:S(2)}, u32[]{:S(2)}) collective-permute-start(f32[5120]{0:T(1024)S(1)} %constant_dynamic-update-slice_fusion), channel_id=1, source_target_pairs={{0,4},{4,0},{1,5},{5,1},{2,6},{6,2},{3,7},{7,3},{8,12},{12,8},{9,1... | collective-permute-start | bytes 61448 | tf_op jit(solution)/shard_map/ppermute | solution.py:49
  325.0 35.2 %collective-permute-start.31 = (bf16[784,512]{1,0:T(8,128)(2,1)S(1)}, bf16[784,512]{1,0:T(8,128)(2,1)S(1)}, u32[]{:S(2)}, u32[]{:S(2)}) collective-permute-start(bf16[784,512]{1,0:T(8,128)(2,1)S(1)} %convert_element_type.384), channel_id=1, source_target_pairs={{0,4},{4,0},{1,5},{5,1},{2,6},{6,2},{3,7},{7,3},{8,12},{12,8},{9,1... | collective-permute-start | bytes 2408456 | tf_op jit(solution)/shard_map/ppermute | solution.py:49
  351.6 3.8 collective-permute-start.43
  353.1 27.5 %collective-permute-start.45 = (bf16[4,128,1024]{2,1,0:T(8,128)(2,1)}, bf16[4,128,1024]{2,1,0:T(8,128)(2,1)}, u32[]{:S(2)}, u32[]{:S(2)}) collective-permute-start(bf16[4,128,1024]{2,1,0:T(8,128)(2,1)} %fusion.51), channel_id=1, source_target_pairs={{0,4},{4,0},{1,5},{5,1},{2,6},{6,2},{3,7},{7,3},{8,12},{12,8},{9,1... | collective-permute-start | bytes 3145736 | tf_op jit(solution)/shard_map/ppermute | solution.py:49
  355.4 4.8 %collective-permute-start.44 = (f32[5120]{0:T(1024)S(1)}, f32[5120]{0:T(1024)S(1)}, u32[]{:S(2)}, u32[]{:S(2)}) collective-permute-start(f32[5120]{0:T(1024)S(1)} %add.333), channel_id=1, source_target_pairs={{0,16},{8,24},{16,0},{24,8},{1,17},{9,25},{17,1},{25,9},{2,18},{10... | collective-permute-start | bytes 61448 | tf_op jit(solution)/shard_map/ppermute | solution.py:115
  363.5 29.8 %collective-permute-start.32 = (bf16[392,1024]{1,0:T(8,128)(2,1)}, bf16[392,1024]{1,0:T(8,128)(2,1)}, u32[]{:S(2)}, u32[]{:S(2)}) collective-permute-start(bf16[392,1024]{1,0:T(8,128)(2,1)} %constant_dynamic-slice_fusion.4), channel_id=1, source_target_pairs={{0,1},{1,0},{2,3},{3,2},{4,5},{5,4},{6,7},{7,6},{8,9},{9,8},{10,11... | collective-permute-start | bytes 2408456 | tf_op jit(solution)/shard_map/ppermute | solution.py:103
  379.6 25.6 %collective-permute-start.35 = (bf16[4,128,1024]{1,2,0:T(8,128)(2,1)S(1)}, bf16[4,128,1024]{1,2,0:T(8,128)(2,1)S(1)}, u32[]{:S(2)}, u32[]{:S(2)}) collective-permute-start(bf16[4,128,1024]{1,2,0:T(8,128)(2,1)S(1)} %bitcast.202), channel_id=1, source_target_pairs={{0,4},{4,0},{1,5},{5,1},{2,6},{6,2},{3,7},{7,3},{8,12},{12,8},{9,1... | collective-permute-start | bytes 3145736 | tf_op jit(solution)/shard_map/ppermute | solution.py:49
  382.6 10.5 %collective-permute-start.46 = (bf16[128,1024]{1,0:T(8,128)(2,1)S(1)}, bf16[128,1024]{1,0:T(8,128)(2,1)S(1)}, u32[]{:S(2)}, u32[]{:S(2)}) collective-permute-start(bf16[128,1024]{1,0:T(8,128)(2,1)S(1)} %fusion.66), channel_id=1, source_target_pairs={{0,8},{8,16},{16,24},{24,0},{1,9},{9,17},{17,25},{25,1},{2,10},{10... | collective-permute-start | bytes 786440 | tf_op jit(solution)/shard_map/ppermute | solution.py:71
  393.2 13.3 %collective-permute-start.47 = (bf16[128,1024]{1,0:T(8,128)(2,1)S(1)}, bf16[128,1024]{1,0:T(8,128)(2,1)S(1)}, u32[]{:S(2)}, u32[]{:S(2)}) collective-permute-start(bf16[128,1024]{1,0:T(8,128)(2,1)S(1)} %fusion.59), channel_id=1, source_target_pairs={{0,8},{8,16},{16,24},{24,0},{1,9},{9,17},{17,25},{25,1},{2,10},{10... | collective-permute-start | bytes 786440 | tf_op jit(solution)/shard_map/ppermute | solution.py:71
  394.7 22.0 %collective-permute-start.33 = (bf16[392,1024]{1,0:T(8,128)(2,1)S(1)}, bf16[392,1024]{1,0:T(8,128)(2,1)S(1)}, u32[]{:S(2)}, u32[]{:S(2)}) collective-permute-start(bf16[392,1024]{1,0:T(8,128)(2,1)S(1)} %add_convert_fusion.3), channel_id=1, source_target_pairs={{0,2},{2,0},{1,3},{3,1},{4,6},{6,4},{5,7},{7,5},{8,10},{10,8},{9,1... | collective-permute-start | bytes 2408456 | tf_op jit(solution)/shard_map/ppermute | solution.py:105
  405.4 11.1 %collective-permute-start.36 = (bf16[128,1024]{0,1:T(8,128)(2,1)S(1)}, bf16[128,1024]{0,1:T(8,128)(2,1)S(1)}, u32[]{:S(2)}, u32[]{:S(2)}) collective-permute-start(bf16[128,1024]{0,1:T(8,128)(2,1)S(1)} %fusion.65), channel_id=1, source_target_pairs={{0,8},{8,16},{16,24},{24,0},{1,9},{9,17},{17,25},{25,1},{2,10},{10... | collective-permute-start | bytes 786440 | tf_op jit(solution)/shard_map/ppermute | solution.py:71
  406.5 20.2 %collective-permute-start.48 = (bf16[128,1024]{1,0:T(8,128)(2,1)S(1)}, bf16[128,1024]{1,0:T(8,128)(2,1)S(1)}, u32[]{:S(2)}, u32[]{:S(2)}) collective-permute-start(bf16[128,1024]{1,0:T(8,128)(2,1)S(1)} %fusion.60), channel_id=1, source_target_pairs={{0,8},{8,16},{16,24},{24,0},{1,9},{9,17},{17,25},{25,1},{2,10},{10... | collective-permute-start | bytes 786440 | tf_op jit(solution)/shard_map/ppermute | solution.py:71
  416.6 9.9 %collective-permute-start.37 = (bf16[128,1024]{0,1:T(8,128)(2,1)S(1)}, bf16[128,1024]{0,1:T(8,128)(2,1)S(1)}, u32[]{:S(2)}, u32[]{:S(2)}) collective-permute-start(bf16[128,1024]{0,1:T(8,128)(2,1)S(1)} %fusion.61), channel_id=1, source_target_pairs={{0,8},{8,16},{16,24},{24,0},{1,9},{9,17},{17,25},{25,1},{2,10},{10... | collective-permute-start | bytes 786440 | tf_op jit(solution)/shard_map/ppermute | solution.py:71
  417.0 18.5 %collective-permute-start.34 = (bf16[392,1024]{1,0:T(8,128)(2,1)S(1)}, bf16[392,1024]{1,0:T(8,128)(2,1)S(1)}, u32[]{:S(2)}, u32[]{:S(2)}) collective-permute-start(bf16[392,1024]{1,0:T(8,128)(2,1)S(1)} %add_convert_fusion.2), channel_id=1, source_target_pairs={{0,1},{1,0},{2,3},{3,2},{4,5},{5,4},{6,7},{7,6},{8,9},{9,8},{10,11... | collective-permute-start | bytes 2408456 | tf_op jit(solution)/shard_map/ppermute | solution.py:107
  426.5 8.9 %collective-permute-start.38 = (bf16[128,1024]{0,1:T(8,128)(2,1)S(1)}, bf16[128,1024]{0,1:T(8,128)(2,1)S(1)}, u32[]{:S(2)}, u32[]{:S(2)}) collective-permute-start(bf16[128,1024]{0,1:T(8,128)(2,1)S(1)} %fusion.62), channel_id=1, source_target_pairs={{0,8},{8,16},{16,24},{24,0},{1,9},{9,17},{17,25},{25,1},{2,10},{10... | collective-permute-start | bytes 786440 | tf_op jit(solution)/shard_map/ppermute | solution.py:71
  438.5 4.4 collective-permute-start.39
  442.9 3.8 collective-permute-start.40
  446.7 9.0 %collective-permute-start.41 = (f32[2560]{0:T(1024)S(1)}, f32[2560]{0:T(1024)S(1)}, u32[]{:S(2)}, u32[]{:S(2)}) collective-permute-start(f32[2560]{0:T(1024)S(1)} %add.330), channel_id=1, source_target_pairs={{0,16},{8,24},{16,0},{24,8},{1,17},{9,25},{17,1},{25,9},{2,18},{10... | collective-permute-start | bytes 30728 | tf_op jit(solution)/shard_map/ppermute | solution.py:115
  (66 other events, 608.3 us)
